TPU v7x, 32 devices: a whole 2x2x4 slice. The times are simulated.
32 devices in a mesh: dp: 8 (over y, x, core), ctx: 4 (over z).
Axes of the slice: x: 2, y: 2, z: 4, core: 2. Of those that a mesh axis runs over, the one named last changes fastest.
Arguments:
- tokens: bfloat16 [16, 1024, 1024], P('dp', 'ctx'), may hold values from -6 to 6
- segments: int32 [16, 1024], P('dp'), may hold values from 0 to 6, as said below
- positions: int32 [16, 1024], P('dp', 'ctx'), may hold values from 0 to 1226, as said below
- attn_gain: bfloat16 [1024], P(('dp', 'ctx')), may hold values from 0.5 to 1.5
- w_query: bfloat16 [1024, 2048], P(('dp', 'ctx')), may hold values from -0.1875 to 0.1875
- w_key: bfloat16 [1024, 1024], P(('dp', 'ctx')), may hold values from -0.1875 to 0.1875
- w_value: bfloat16 [1024, 1024], P(('dp', 'ctx')), may hold values from -0.1875 to 0.1875
- w_out: bfloat16 [1024, 2048], P(('dp', 'ctx')), may hold values from -0.5 to 0.5
- qk_gain: bfloat16 [2, 128], replicated, may hold values from 0.25 to 1.75
- mlp_gain: bfloat16 [1024], P(('dp', 'ctx')), may hold values from 0.5 to 1.5
- w_gate: bfloat16 [1024, 3072], P(('dp', 'ctx')), may hold values from -0.1875 to 0.1875
- w_up: bfloat16 [1024, 3072], P(('dp', 'ctx')), may hold values from -0.1875 to 0.1875
- w_down: bfloat16 [1024, 3072], P(('dp', 'ctx')), may hold values from -0.21875 to 0.21875
- cotangent: bfloat16 [16, 1024, 1024], P('dp', 'ctx'), may hold values from -6 to 6
Outputs:
- layer_out: bfloat16 [16, 1024, 1024], P('dp', 'ctx')
- d_tokens: float32 [16, 1024, 1024], P('dp', 'ctx')
- d_attn_gain: float32 [1024], P(('dp', 'ctx'))
- d_w_query: float32 [1024, 2048], P(('dp', 'ctx'))
- d_w_key: float32 [1024, 1024], P(('dp', 'ctx'))
- d_w_value: float32 [1024, 1024], P(('dp', 'ctx'))
- d_w_out: float32 [1024, 2048], P(('dp', 'ctx'))
- d_qk_gain: float32 [2, 128], replicated
- d_mlp_gain: float32 [1024], P(('dp', 'ctx'))
- d_w_gate: float32 [1024, 3072], P(('dp', 'ctx'))
- d_w_up: float32 [1024, 3072], P(('dp', 'ctx'))
- d_w_down: float32 [1024, 3072], P(('dp', 'ctx'))
Inputs may be any that keep to these rules, and one draw needn't show every extreme that they name: `segments`: numbers start at 0 in every sequence and rise by one at the first token of each further document; every document holds 204 tokens or more, counting those before the sequence, except the last document of a sequence, which may be cut off by its end. `positions`: A token's position counts from its document's first token; a sequence's first document may have begun up to 203 tokens before the sequence.
All inputs are finite; a program needn't handle non-finite values.
Results may differ from a plain program's by a relative error of at most 0.017.
Values may be sent and summed in bfloat16 or wider, within the bound.
No kernel may reach another device: no remote copies, remote signals or barrier semaphores. Data moves between devices by JAX's collectives and lax.ppermute only.
A program may use at most 256 MiB of HBM per device.

v0:
```python
import jax
import jax.numpy as jnp
from jax import lax
from jax.sharding import PartitionSpec as P

D = 1024
HQ = 16
HK = 8
DH = 128


norm_eps = 1e-06
rope_base = 1000000.0


def norm_rows(values, gain):
    factor = lax.rsqrt(jnp.mean(values * values, axis=-1, keepdims=True) + norm_eps)
    return (values * factor * gain, factor)


def norm_back(values, factor, gain, upstream):
    weighted = upstream * gain
    lead_axes = tuple(range(values.ndim - 1))
    gain_grad = jnp.sum(upstream * values * factor, axis=lead_axes)
    inner_mean = jnp.mean(weighted * values, axis=-1, keepdims=True)
    return (gain_grad, factor * weighted - values * factor * factor * factor * inner_mean)


def rotate(values, positions, sign):
    half_dim = values.shape[-1] // 2
    inv_freq = rope_base ** (-2.0 * jnp.arange(half_dim, dtype=jnp.float32) / values.shape[-1])
    angles = positions.astype(jnp.float32)[:, None, None] * inv_freq
    cosine = jnp.cos(angles)
    sine = sign * jnp.sin(angles)
    first_half = values[..., :half_dim]
    second_half = values[..., half_dim:]
    return jnp.concatenate(
        [first_half * cosine - second_half * sine, second_half * cosine + first_half * sine],
        axis=-1,
    )


def visibility(segment_row, q_first, span_len):
    key_places = jnp.arange(segment_row.shape[0], dtype=jnp.int32)
    query_places = q_first + jnp.arange(span_len, dtype=jnp.int32)
    query_segs = lax.dynamic_slice_in_dim(segment_row, q_first, span_len)
    return (query_segs[:, None] == segment_row[None, :]) & (
        key_places[None, :] <= query_places[:, None]
    )


def masked_scores(grouped, keys, visible):
    scores = jnp.einsum(
        "qhgd,khd->hgqk", grouped, keys, preferred_element_type=jnp.float32
    ) * DH ** (-0.5)
    return jnp.where(visible, scores, -1e30)


def local(
    tokens,
    segments,
    positions,
    attn_gain,
    w_query,
    w_key,
    w_value,
    w_out,
    qk_gain,
    mlp_gain,
    w_gate,
    w_up,
    w_down,
    cotangent,
):
    seq_count, span_len, _ = tokens.shape
    row_count = seq_count * span_len
    heads_per = HQ // HK
    q_first = lax.axis_index("ctx") * span_len
    pos_flat = positions.reshape(row_count)
    g_attn, wq_full, wk_full, wv_full, wo_full = (
        lax.all_gather(attn_gain, ("dp", "ctx"), axis=0, tiled=True),
        lax.all_gather(w_query, ("dp", "ctx"), axis=0, tiled=True),
        lax.all_gather(w_key, ("dp", "ctx"), axis=0, tiled=True),
        lax.all_gather(w_value, ("dp", "ctx"), axis=0, tiled=True),
        lax.all_gather(w_out, ("dp", "ctx"), axis=0, tiled=True),
    )
    resid_in = tokens.reshape(row_count, D).astype(jnp.float32)
    normed_f, factor_in = norm_rows(resid_in, g_attn.astype(jnp.float32))
    normed = normed_f.astype(jnp.bfloat16)
    q_proj = jnp.dot(normed, wq_full, preferred_element_type=jnp.float32).reshape(row_count, HQ, DH)
    k_proj = jnp.dot(normed, wk_full, preferred_element_type=jnp.float32).reshape(row_count, HK, DH)
    v_low = (
        jnp.dot(normed, wv_full, preferred_element_type=jnp.float32)
        .astype(jnp.bfloat16)
        .reshape(seq_count, span_len, HK, DH)
    )
    gains_qk = qk_gain.astype(jnp.float32)
    q_norm, factor_q = norm_rows(q_proj, gains_qk[0])
    k_norm, factor_k = norm_rows(k_proj, gains_qk[1])
    q_low = rotate(q_norm, pos_flat, 1.0).astype(jnp.bfloat16).reshape(seq_count, span_len, HQ, DH)
    k_low = rotate(k_norm, pos_flat, 1.0).astype(jnp.bfloat16).reshape(seq_count, span_len, HK, DH)
    keys_all, values_all = (
        lax.all_gather(k_low, "ctx", axis=1, tiled=True),
        lax.all_gather(v_low, "ctx", axis=1, tiled=True),
    )

    def attend_forward(group_item):
        queries, keys, values, segment_row = group_item
        visible = visibility(segment_row, q_first, span_len)
        grouped = queries.reshape(span_len, HK, heads_per, DH)
        scores = masked_scores(grouped, keys, visible)
        row_max = jnp.max(scores, axis=-1, keepdims=True)
        weights = jnp.exp(scores - row_max)
        row_total = jnp.sum(weights, axis=-1, keepdims=True)
        prob_low = (weights / row_total).astype(jnp.bfloat16)
        attn_mix = jnp.einsum(
            "hgqk,khd->qhgd", prob_low, values, preferred_element_type=jnp.float32
        )
        return (
            attn_mix.reshape(span_len, HQ * DH).astype(jnp.bfloat16),
            row_max + jnp.log(row_total),
        )

    attn_mix, log_total = lax.map(attend_forward, (q_low, keys_all, values_all, segments))
    attn_mix = attn_mix.reshape(row_count, HQ * DH)
    hidden_in = resid_in + jnp.einsum(
        "th,dh->td", attn_mix, wo_full, preferred_element_type=jnp.float32
    )
    g_mlp, wg_full, wu_full, wd_full = (
        lax.all_gather(mlp_gain, ("dp", "ctx"), axis=0, tiled=True),
        lax.all_gather(w_gate, ("dp", "ctx"), axis=0, tiled=True),
        lax.all_gather(w_up, ("dp", "ctx"), axis=0, tiled=True),
        lax.all_gather(w_down, ("dp", "ctx"), axis=0, tiled=True),
    )
    normed_mlp_f, factor_mlp = norm_rows(hidden_in, g_mlp.astype(jnp.float32))
    normed_mlp = normed_mlp_f.astype(jnp.bfloat16)
    gated = jnp.dot(normed_mlp, wg_full, preferred_element_type=jnp.float32)
    upward = jnp.dot(normed_mlp, wu_full, preferred_element_type=jnp.float32)
    sigmoid_gate = jax.nn.sigmoid(gated)
    silu_gate = gated * sigmoid_gate
    inner = (silu_gate * upward).astype(jnp.bfloat16)
    result = hidden_in + jnp.einsum("tf,df->td", inner, wd_full, preferred_element_type=jnp.float32)
    layer_out = result.astype(jnp.bfloat16).reshape(seq_count, span_len, D)
    g_mlp, wg_full, wu_full, wd_full = (
        lax.all_gather(mlp_gain, ("dp", "ctx"), axis=0, tiled=True),
        lax.all_gather(w_gate, ("dp", "ctx"), axis=0, tiled=True),
        lax.all_gather(w_up, ("dp", "ctx"), axis=0, tiled=True),
        lax.all_gather(w_down, ("dp", "ctx"), axis=0, tiled=True),
    )
    grad_out = cotangent.reshape(row_count, D)
    grad_inner = jnp.dot(grad_out, wd_full, preferred_element_type=jnp.float32)
    grad_gate = (grad_inner * upward * sigmoid_gate * (1.0 + gated * (1.0 - sigmoid_gate))).astype(
        jnp.bfloat16
    )
    grad_up = (grad_inner * silu_gate).astype(jnp.bfloat16)
    grad_normed_mlp = jnp.einsum(
        "tf,df->td", grad_gate, wg_full, preferred_element_type=jnp.float32
    )
    grad_normed_mlp = grad_normed_mlp + jnp.einsum(
        "tf,df->td", grad_up, wu_full, preferred_element_type=jnp.float32
    )
    mlp_gain_part, grad_resid_mlp = norm_back(
        hidden_in, factor_mlp, g_mlp.astype(jnp.float32), grad_normed_mlp
    )
    d_w_down = jnp.einsum("td,tf->df", grad_out, inner, preferred_element_type=jnp.float32)
    d_w_gate = jnp.einsum("td,tf->df", normed_mlp, grad_gate, preferred_element_type=jnp.float32)
    d_w_up = jnp.einsum("td,tf->df", normed_mlp, grad_up, preferred_element_type=jnp.float32)
    d_mlp_gain, d_w_gate, d_w_up, d_w_down = (
        lax.psum_scatter(mlp_gain_part, ("dp", "ctx"), scatter_dimension=0, tiled=True),
        lax.psum_scatter(d_w_gate, ("dp", "ctx"), scatter_dimension=0, tiled=True),
        lax.psum_scatter(d_w_up, ("dp", "ctx"), scatter_dimension=0, tiled=True),
        lax.psum_scatter(d_w_down, ("dp", "ctx"), scatter_dimension=0, tiled=True),
    )
    grad_hidden = grad_out.astype(jnp.float32) + grad_resid_mlp
    g_attn, wq_full, wk_full, wv_full, wo_full = (
        lax.all_gather(attn_gain, ("dp", "ctx"), axis=0, tiled=True),
        lax.all_gather(w_query, ("dp", "ctx"), axis=0, tiled=True),
        lax.all_gather(w_key, ("dp", "ctx"), axis=0, tiled=True),
        lax.all_gather(w_value, ("dp", "ctx"), axis=0, tiled=True),
        lax.all_gather(w_out, ("dp", "ctx"), axis=0, tiled=True),
    )
    grad_attn = grad_hidden.astype(jnp.bfloat16)
    grad_mix = jnp.einsum(
        "td,dh->th", grad_attn, wo_full, preferred_element_type=jnp.float32
    ).astype(jnp.bfloat16)
    grad_mix = grad_mix.reshape(seq_count, span_len, HQ, DH)

    def attend_backward(group_item):
        queries, keys, values, grad_rows, log_rows, segment_row = group_item
        visible = visibility(segment_row, q_first, span_len)
        grouped = queries.reshape(span_len, HK, heads_per, DH)
        scores = masked_scores(grouped, keys, visible)
        probs = jnp.exp(scores - log_rows)
        grad_group = grad_rows.reshape(span_len, HK, heads_per, DH)
        grad_probs = jnp.einsum(
            "qhgd,khd->hgqk", grad_group, values, preferred_element_type=jnp.float32
        )
        center = jnp.sum(probs * grad_probs, axis=-1, keepdims=True)
        grad_scores = (probs * (grad_probs - center)).astype(jnp.bfloat16)
        grad_q = jnp.einsum(
            "hgqk,khd->qhgd", grad_scores, keys, preferred_element_type=jnp.float32
        ) * DH ** (-0.5)
        grad_k = jnp.einsum(
            "hgqk,qhgd->khd", grad_scores, grouped, preferred_element_type=jnp.float32
        ) * DH ** (-0.5)
        grad_v = jnp.einsum(
            "hgqk,qhgd->khd",
            probs.astype(jnp.bfloat16),
            grad_group,
            preferred_element_type=jnp.float32,
        )
        return (grad_q.reshape(span_len, HQ, DH), grad_k, grad_v)

    grad_q, grad_k_all, grad_v_all = lax.map(
        attend_backward, (q_low, keys_all, values_all, grad_mix, log_total, segments)
    )
    grad_k, grad_v = (
        lax.psum_scatter(
            grad_k_all.astype(jnp.bfloat16), "ctx", scatter_dimension=1, tiled=True
        ).astype(jnp.float32),
        lax.psum_scatter(
            grad_v_all.astype(jnp.bfloat16), "ctx", scatter_dimension=1, tiled=True
        ).astype(jnp.float32),
    )
    grad_qn = rotate(grad_q.reshape(row_count, HQ, DH), pos_flat, -1.0)
    grad_kn = rotate(grad_k.reshape(row_count, HK, DH), pos_flat, -1.0)
    q_gain_part, grad_qp = norm_back(q_proj, factor_q, gains_qk[0], grad_qn)
    k_gain_part, grad_kp = norm_back(k_proj, factor_k, gains_qk[1], grad_kn)
    grad_q_low = grad_qp.reshape(row_count, HQ * DH).astype(jnp.bfloat16)
    grad_k_low = grad_kp.reshape(row_count, HK * DH).astype(jnp.bfloat16)
    grad_v_low = grad_v.reshape(row_count, HK * DH).astype(jnp.bfloat16)
    grad_normed = jnp.einsum("th,dh->td", grad_q_low, wq_full, preferred_element_type=jnp.float32)
    grad_normed = grad_normed + jnp.einsum(
        "th,dh->td", grad_k_low, wk_full, preferred_element_type=jnp.float32
    )
    grad_normed = grad_normed + jnp.einsum(
        "th,dh->td", grad_v_low, wv_full, preferred_element_type=jnp.float32
    )
    attn_gain_part, grad_resid_attn = norm_back(
        resid_in, factor_in, g_attn.astype(jnp.float32), grad_normed
    )
    d_qk_gain = lax.psum(jnp.stack([q_gain_part, k_gain_part]), ("dp", "ctx"))
    d_w_out = jnp.einsum("td,th->dh", grad_attn, attn_mix, preferred_element_type=jnp.float32)
    d_w_query = jnp.einsum("td,th->dh", normed, grad_q_low, preferred_element_type=jnp.float32)
    d_w_key = jnp.einsum("td,th->dh", normed, grad_k_low, preferred_element_type=jnp.float32)
    d_w_value = jnp.einsum("td,th->dh", normed, grad_v_low, preferred_element_type=jnp.float32)
    d_attn_gain, d_w_query, d_w_key, d_w_value, d_w_out = (
        lax.psum_scatter(attn_gain_part, ("dp", "ctx"), scatter_dimension=0, tiled=True),
        lax.psum_scatter(d_w_query, ("dp", "ctx"), scatter_dimension=0, tiled=True),
        lax.psum_scatter(d_w_key, ("dp", "ctx"), scatter_dimension=0, tiled=True),
        lax.psum_scatter(d_w_value, ("dp", "ctx"), scatter_dimension=0, tiled=True),
        lax.psum_scatter(d_w_out, ("dp", "ctx"), scatter_dimension=0, tiled=True),
    )
    d_tokens = (grad_hidden + grad_resid_attn).reshape(seq_count, span_len, D)
    return (
        layer_out,
        d_tokens,
        d_attn_gain,
        d_w_query,
        d_w_key,
        d_w_value,
        d_w_out,
        d_qk_gain,
        d_mlp_gain,
        d_w_gate,
        d_w_up,
        d_w_down,
    )


def solution(mesh):
    in_specs = (
        P("dp", "ctx", None),
        P("dp", None),
        P("dp", "ctx"),
        P(("dp", "ctx")),
        P(("dp", "ctx"), None),
        P(("dp", "ctx"), None),
        P(("dp", "ctx"), None),
        P(("dp", "ctx"), None),
        P(),
        P(("dp", "ctx")),
        P(("dp", "ctx"), None),
        P(("dp", "ctx"), None),
        P(("dp", "ctx"), None),
        P("dp", "ctx", None),
    )
    out_specs = (
        P("dp", "ctx", None),
        P("dp", "ctx", None),
        P(("dp", "ctx")),
        P(("dp", "ctx"), None),
        P(("dp", "ctx"), None),
        P(("dp", "ctx"), None),
        P(("dp", "ctx"), None),
        P(),
        P(("dp", "ctx")),
        P(("dp", "ctx"), None),
        P(("dp", "ctx"), None),
        P(("dp", "ctx"), None),
    )
    return jax.shard_map(local, mesh=mesh, in_specs=in_specs, out_specs=out_specs, check_vma=False)
```

profile of v0, /device:TPU:0, one launch (start us, length us, event | category | flops | bytes accessed | tf_op | source)
XLA Modules:
  0.0 2191.9 jit_solution(18312175057092904300)
XLA Ops:
  11.1 42.0 %all-reduce.5 = (bf16[1024]{0:T(1024)(128)(2,1)S(1)}, bf16[1024]{0:T(1024)(128)(2,1)S(1)}) all-reduce(bf16[1024]{0:T(1024)(128)(2,1)S(1)} %dynamic-update-slice, bf16[1024]{0:T(1024)(128)(2,1)S(1)} %dynamic-update-slice.1), channel_id=1, replica_groups=mesh['dp'=8,'ctx'=4] {'dp','ctx'}, use_global_device_ids=true, to_apply=%add | all-reduce | flops 2048 | bytes 8192
  56.8 13.3 all-gather.10.cloned.1.call-done
  76.2 52.3 %all-gather.14.cloned.1.call-done = bf16[1024,1024]{1,0:T(8,128)(2,1)} async-done(((bf16[32,1024]{1,0:T(8,128)(2,1)}), bf16[1024,1024]{1,0:T(8,128)(2,1)}) %all-gather.14.cloned.1.call-update) | async-done | bytes 2097168 | tf_op jit(solution)/shard_map/all_gather | solution.py:83
  140.9 51.5 %all-gather.18.cloned.1.call-done = bf16[1024,2048]{1,0:T(8,128)(2,1)} async-done(((bf16[32,2048]{1,0:T(8,128)(2,1)}), bf16[1024,2048]{1,0:T(8,128)(2,1)}) %all-gather.18.cloned.1.call-update) | async-done | bytes 4194320 | tf_op jit(solution)/shard_map/all_gather | solution.py:82
  219.9 53.9 %all-gather.12.cloned.1.call-done = bf16[2,1024,8,128]{3,1,2,0:T(8,128)(2,1)} async-done(((bf16[2,256,8,128]{3,1,2,0:T(8,128)(2,1)}), bf16[2,1024,8,128]{3,1,2,0:T(8,128)(2,1)}) %all-gather.12.cloned.1.call-update) | async-done | bytes 4194320 | tf_op jit(solution)/shard_map/all_gather | solution.py:104
  273.8 80.7 %all-gather.16.cloned.1.call-done = bf16[2,1024,8,128]{3,1,2,0:T(8,128)(2,1)} async-done(((bf16[2,256,8,128]{3,1,2,0:T(8,128)(2,1)}), bf16[2,1024,8,128]{3,1,2,0:T(8,128)(2,1)}) %all-gather.16.cloned.1.call-update) | async-done | bytes 4194320 | tf_op jit(solution)/shard_map/all_gather | solution.py:103
  354.6 61.7 %while.32 = (s32[]{:T(128)}, bf16[2,256,2048]{2,1,0:T(8,128)(2,1)}, f32[2,8,2,256,1]{3,2,1,4,0:T(2,128)S(1)}, bf16[2,1024,8,128]{3,1,2,0:T(8,128)(2,1)}, s32[2,1...) while((s32[]{:T(128)}, bf16[2,256,2048]{2,1,0:T(8,128)(2,1)}, ...), condition=%wide.region_6.7_spmd, body=%wide.region_3.6_spmd.sunk | while | flops 2199122176 | bytes 64111780 | solution.py:124
  395.8 9.7 fusion.143
  423.7 65.4 %all-gather.22.cloned.1.call-done = bf16[1024,3072]{1,0:T(8,128)(2,1)} async-done(((bf16[32,3072]{1,0:T(8,128)(2,1)}), bf16[1024,3072]{1,0:T(8,128)(2,1)}) %all-gather.22.cloned.1.call-update) | async-done | bytes 6291472 | tf_op jit(solution)/shard_map/all_gather | solution.py:131
  497.2 62.9 %all-gather.24.cloned.1.call-done = bf16[1024,3072]{1,0:T(8,128)(2,1)} async-done(((bf16[32,3072]{1,0:T(8,128)(2,1)}), bf16[1024,3072]{1,0:T(8,128)(2,1)}) %all-gather.24.cloned.1.call-update) | async-done | bytes 6291472 | tf_op jit(solution)/shard_map/all_gather | solution.py:132
  568.6 62.4 %all-gather.26.cloned.1.call-done = bf16[1024,3072]{1,0:T(8,128)(2,1)} async-done(((bf16[32,3072]{1,0:T(8,128)(2,1)}), bf16[1024,3072]{1,0:T(8,128)(2,1)}) %all-gather.26.cloned.1.call-update) | async-done | bytes 6291472 | tf_op jit(solution)/shard_map/all_gather | solution.py:133
  631.1 11.8 multiply_convert_fusion
  661.7 209.1 %while.33 = (s32[]{:T(128)}, f32[2,256,16,128]{1,0,3,2:T(2,128)}, bf16[2,1024,8,128]{1,3,2,0:T(8,128)(2,1)}, bf16[2,1024,8,128]{1,3,2,0:T(8,128)(2,1)}, bf16[2,1...) while((s32[]{:T(128)}, f32[2,256,16,128]{1,0,3,2:T(2,128)}, ...), condition=%wide.region_11.12_spmd, body=%wide.region_9.11_spmd.sunk | while | flops 5408813056 | bytes 262767968 | solution.py:214
  674.1 12.2 fusion.156
  686.4 11.7 fusion.157
  704.9 42.7 %dynamic_update_slice.52 = f32[2,256,16,128]{1,0,3,2:T(2,128)} dynamic-update-slice(f32[2,256,16,128]{1,0,3,2:T(2,128)} %get-tuple-element.716, f32[1,256,16,128]{1,0,3,2:T(1,128)} %copy.141, s32[]{:T(128)S(6)} %copy.162, s32[]{:T(128)} %constant.196.clone.1..sunk.1, s32[]{:T(128)} %constant.196.clone.1..sunk.1, s32[]{:T(128)} %constant.196.clone.1..sunk.1) | dynamic-update-slice | bytes 4194308 | tf_op jit(solution)/shard_map/while/body/jit(dynamic_update_index_in_dim)/dynamic_update_slice | solution.py:214
  778.5 12.2 fusion.156
  790.7 11.7 fusion.157
  809.3 42.7 %dynamic_update_slice.52 = f32[2,256,16,128]{1,0,3,2:T(2,128)} dynamic-update-slice(f32[2,256,16,128]{1,0,3,2:T(2,128)} %get-tuple-element.716, f32[1,256,16,128]{1,0,3,2:T(1,128)} %copy.141, s32[]{:T(128)S(6)} %copy.162, s32[]{:T(128)} %constant.196.clone.1..sunk.1, s32[]{:T(128)} %constant.196.clone.1..sunk.1, s32[]{:T(128)} %constant.196.clone.1..sunk.1) | dynamic-update-slice | bytes 4194308 | tf_op jit(solution)/shard_map/while/body/jit(dynamic_update_index_in_dim)/dynamic_update_slice | solution.py:214
  901.3 10.2 fusion.72
  911.6 10.2 fusion.73
  921.9 10.1 convolution_bitcast_fusion
  932.1 12.7 copy.102
  955.9 70.0 %reduce-scatter.14.cloned.1.call-done = bf16[2,256,8,128]{1,3,2,0:T(8,128)(2,1)} async-done(((bf16[2,1024,8,128]{1,3,2,0:T(8,128)(2,1)}), bf16[2,256,8,128]{1,3,2,0:T(8,128)(2,1)}) %reduce-scatter.14.cloned.1.call-update) | async-done | bytes 1048592 | tf_op jit(solution)/shard_map/reduce_scatter | solution.py:221
  1051.4 43.7 %all-reduce.4 = (f32[1024]{0:T(1024)S(1)}, f32[2,128]{1,0:T(2,128)}, f32[1024]{0:T(1024)S(1)}) all-reduce(f32[1024]{0:T(1024)S(1)} %get-tuple-element.453, f32[2,128]{1,0:T(2,128)S(1)} %pad_maximum_fusion.4, f32[1024]{0:T(1024)S(1)} %copy-done.44), channel_id=4, replica_groups=mesh['dp'=8,'ctx'=4] {'dp','ctx'}, use_global_device_ids=true, to_apply=%region_18.19.clone | all-reduce | flops 2304 | bytes 18432
  1099.9 116.2 %reduce-scatter.16.cloned.1.call-done = f32[32,2048]{1,0:T(8,128)} async-done(((f32[1024,2048]{1,0:T(8,128)}), f32[32,2048]{1,0:T(8,128)}) %reduce-scatter.16.cloned.1.call-update) | async-done | bytes 262160 | tf_op jit(solution)/shard_map/reduce_scatter | solution.py:249
  1216.1 186.3 %reduce-scatter.22.cloned.1.call-done = f32[32,2048]{1,0:T(8,128)} async-done(((f32[1024,2048]{1,0:T(8,128)}), f32[32,2048]{1,0:T(8,128)}) %reduce-scatter.22.cloned.1.call-update) | async-done | bytes 262160 | tf_op jit(solution)/shard_map/reduce_scatter | solution.py:252
  1402.4 159.5 %reduce-scatter.24.cloned.1.call-done = f32[32,3072]{1,0:T(8,128)} async-done(((f32[1024,3072]{1,0:T(8,128)}), f32[32,3072]{1,0:T(8,128)}) %reduce-scatter.24.cloned.1.call-update) | async-done | bytes 393232 | tf_op jit(solution)/shard_map/reduce_scatter | solution.py:170
  1561.9 162.0 %reduce-scatter.26.cloned.1.call-done = f32[32,3072]{1,0:T(8,128)} async-done(((f32[1024,3072]{1,0:T(8,128)}), f32[32,3072]{1,0:T(8,128)}) %reduce-scatter.26.cloned.1.call-update) | async-done | bytes 393232 | tf_op jit(solution)/shard_map/reduce_scatter | solution.py:171
  1723.9 161.2 %reduce-scatter.28.cloned.1.call-done = f32[32,3072]{1,0:T(8,128)} async-done(((f32[1024,3072]{1,0:T(8,128)}), f32[32,3072]{1,0:T(8,128)}) %reduce-scatter.28.cloned.1.call-update) | async-done | bytes 393232
  1885.1 149.7 %reduce-scatter.18.cloned.1.call-done = f32[32,1024]{1,0:T(8,128)} async-done(((f32[1024,1024]{1,0:T(8,128)}), f32[32,1024]{1,0:T(8,128)}) %reduce-scatter.18.cloned.1.call-update) | async-done | bytes 131088 | tf_op jit(solution)/shard_map/reduce_scatter | solution.py:250
  2034.8 150.0 %reduce-scatter.20.cloned.1.call-done = f32[32,1024]{1,0:T(8,128)} async-done(((f32[1024,1024]{1,0:T(8,128)}), f32[32,1024]{1,0:T(8,128)}) %reduce-scatter.20.cloned.1.call-update) | async-done | bytes 131088 | tf_op jit(solution)/shard_map/reduce_scatter | solution.py:251
  (280 shorter events, 294.2 us)
Async XLA Ops:
  7.2 63.0 %all-gather.10.cloned.1.call-start = ((), (), s32[]{:S(2)}) async-start(), calls=%async_computation.9 | async-start | bytes 2162688 | tf_op jit(solution)/shard_map/all_gather | solution.py:84
  7.9 120.6 %all-gather.14.cloned.1.call-start = ((), (), s32[]{:S(2)}) async-start(), calls=%async_computation.11 | async-start | bytes 2162688 | tf_op jit(solution)/shard_map/all_gather | solution.py:83
  8.7 183.8 %all-gather.18.cloned.1.call-start = ((), (), s32[]{:S(2)}) async-start(), calls=%async_computation.13 | async-start | bytes 4325376 | tf_op jit(solution)/shard_map/all_gather | solution.py:82
  9.4 264.4 %all-gather.12.cloned.1.call-start = ((), (), s32[]{:S(2)}) async-start(), calls=%async_computation.10 | async-start | bytes 5242880 | tf_op jit(solution)/shard_map/all_gather | solution.py:104
  53.2 22.7 %copy-start.35 = (f32[1024]{0:T(1024)}, f32[1024]{0:T(1024)S(1)}, u32[]{:S(2)}) copy-start(f32[1024]{0:T(1024)S(1)} %convert_element_type.152) | copy-start | bytes 12292
  74.5 280.0 %all-gather.16.cloned.1.call-start = ((), (), s32[]{:S(2)}) async-start(), calls=%async_computation.12 | async-start | bytes 5242880 | tf_op jit(solution)/shard_map/all_gather | solution.py:103
  74.7 58.1 %copy-start.40 = (f32[128]{0:T(128)}, f32[128]{0:T(128)S(1)}, u32[]{:S(2)}) copy-start(f32[128]{0:T(128)S(1)} %get-tuple-element.523) | copy-start | bytes 1540
  74.7 129.4 %copy-start.42 = (f32[128]{0:T(128)}, f32[128]{0:T(128)S(1)}, u32[]{:S(2)}) copy-start(f32[128]{0:T(128)S(1)} %get-tuple-element.522) | copy-start | bytes 1540
  75.9 129.0 %copy-start.16 = (f32[512,64]{0,1:T(8,128)}, f32[512,64]{0,1:T(8,128)S(1)}, u32[]{:S(2)}) copy-start(f32[512,64]{0,1:T(8,128)S(1)} %get-tuple-element.519) | copy-start | bytes 393220
  76.2 56.5 %copy-start.22 = (bf16[2,256,1024]{2,1,0:T(8,128)(2,1)}, bf16[2,256,1024]{2,1,0:T(8,128)(2,1)S(1)}, u32[]{:S(2)}) copy-start(bf16[2,256,1024]{2,1,0:T(8,128)(2,1)S(1)} %fusion.50) | copy-start | bytes 3145732
  137.3 280.8 %all-gather.20.cloned.1.call-start = ((), (), s32[]{:S(2)}) async-start(), calls=%async_computation.14 | async-start | bytes 4325376 | tf_op jit(solution)/shard_map/all_gather | solution.py:85
  137.8 351.3 %all-gather.22.cloned.1.call-start = ((), (), s32[]{:S(2)}) async-start(), calls=%async_computation.15 | async-start | bytes 6488064 | tf_op jit(solution)/shard_map/all_gather | solution.py:131
  138.6 421.5 %all-gather.24.cloned.1.call-start = ((), (), s32[]{:S(2)}) async-start(), calls=%async_computation.16 | async-start | bytes 6488064 | tf_op jit(solution)/shard_map/all_gather | solution.py:132
  139.3 491.7 %all-gather.26.cloned.1.call-start = ((), (), s32[]{:S(2)}) async-start(), calls=%async_computation.17 | async-start | bytes 6488064 | tf_op jit(solution)/shard_map/all_gather | solution.py:133
  140.1 806.2 %reduce-scatter.12.cloned.1.call-start = ((), (), s32[]{:S(2)}) async-start(), calls=%async_computation.18 | async-start | bytes 5242880 | tf_op jit(solution)/shard_map/reduce_scatter | solution.py:218
  215.8 138.7 %copy-start.32 = (s32[2,1024]{1,0:T(2,128)S(1)}, s32[2,1024]{1,0:T(2,128)}, u32[]{:S(2)}) copy-start(s32[2,1024]{1,0:T(2,128)} %param.19) | copy-start | bytes 24580
  354.6 63.5 %copy-start.10 = (bf16[2,256,1024]{2,1,0:T(8,128)(2,1)S(1)}, bf16[2,256,1024]{2,1,0:T(8,128)(2,1)}, u32[]{:S(2)}) copy-start(bf16[2,256,1024]{2,1,0:T(8,128)(2,1)} %param.18) | copy-start | bytes 3145732
  423.4 231.7 %copy-start.12 = (f32[512,1024]{1,0:T(8,128)}, f32[512,1024]{1,0:T(8,128)S(1)}, u32[]{:S(2)}) copy-start(f32[512,1024]{1,0:T(8,128)S(1)} %get-tuple-element.529) | copy-start | bytes 6291460
  423.6 136.4 %copy-start.25 = (bf16[512,1024]{1,0:T(8,128)(2,1)}, bf16[512,1024]{1,0:T(8,128)(2,1)S(1)}, u32[]{:S(2)}) copy-start(bf16[512,1024]{1,0:T(8,128)(2,1)S(1)} %multiply_convert_fusion.3) | copy-start | bytes 3145732
  642.9 7.9 copy-start.46
  686.4 11.8 copy-start.1
  790.7 11.8 copy-start.1
  870.8 155.1 %reduce-scatter.14.cloned.1.call-start = ((), (), s32[]{:S(2)}) async-start(), calls=%async_computation.19 | async-start | bytes 5242880 | tf_op jit(solution)/shard_map/reduce_scatter | solution.py:221
  871.6 344.5 %reduce-scatter.16.cloned.1.call-start = ((), (), s32[]{:S(2)}) async-start(), calls=%async_computation.20 | async-start | bytes 8650752 | tf_op jit(solution)/shard_map/reduce_scatter | solution.py:249
  892.3 510.1 %reduce-scatter.22.cloned.1.call-start = ((), (), s32[]{:S(2)}) async-start(), calls=%async_computation.23 | async-start | bytes 8650752 | tf_op jit(solution)/shard_map/reduce_scatter | solution.py:252
  901.1 660.9 %reduce-scatter.24.cloned.1.call-start = ((), (), s32[]{:S(2)}) async-start(), calls=%async_computation.24 | async-start | bytes 12976128 | tf_op jit(solution)/shard_map/reduce_scatter | solution.py:170
  911.6 812.3 %reduce-scatter.26.cloned.1.call-start = ((), (), s32[]{:S(2)}) async-start(), calls=%async_computation.25 | async-start | bytes 12976128 | tf_op jit(solution)/shard_map/reduce_scatter | solution.py:171
  921.9 963.3 %reduce-scatter.28.cloned.1.call-start = ((), (), s32[]{:S(2)}) async-start(), calls=%async_computation.26 | async-start | bytes 12976128
  944.8 1090.1 %reduce-scatter.18.cloned.1.call-start = ((), (), s32[]{:S(2)}) async-start(), calls=%async_computation.21 | async-start | bytes 4325376 | tf_op jit(solution)/shard_map/reduce_scatter | solution.py:250
  955.7 1229.1 %reduce-scatter.20.cloned.1.call-start = ((), (), s32[]{:S(2)}) async-start(), calls=%async_computation.22 | async-start | bytes 4325376 | tf_op jit(solution)/shard_map/reduce_scatter | solution.py:251
  1032.9 9.1 copy-start.26
  1032.9 9.1 copy-start.48
  (43 other events, 137.6 us)
Sparse Core Ops, SparseCore 0:
  10.9 59.1 all-gather.9
  73.1 55.3 all-gather.13
  131.5 60.9 all-gather.17
  194.5 79.2 all-gather.11
  275.2 79.2 all-gather.15
  357.4 60.6 all-gather.19
  421.0 68.0 all-gather.21
  492.0 68.0 all-gather.23
  563.0 68.0 all-gather.25
  870.9 75.2 reduce-scatter.11
  948.7 77.2 reduce-scatter.13
  1028.7 187.3 reduce-scatter.15
  1218.9 183.4 reduce-scatter.21
  1408.9 153.0 reduce-scatter.23
  1569.4 154.4 reduce-scatter.25
  1730.3 154.7 reduce-scatter.27
  1887.9 146.8 reduce-scatter.17
  2037.6 147.1 reduce-scatter.19
where the time goes:
time: 2210 us; the launch traced here: 2190 us
  waiting for transfers between devices  1610 us (73%)
  matrix products  237 us (11%)
  local copies, waits for them, and re-layouts  174 us (8%)
  blocking collectives  85.7 us (4%)
  other arithmetic  70.9 us (3%)
    reduce_scatter x1, waiting for transfers between devices, local(): lax.psum_scatter(d_w_out, ('dp', 'ctx'), scatter_dimension=0, tiled=True)  186 us
    unnamed x19, waiting for transfers between devices  167 us
    reduce_scatter x1, waiting for transfers between devices, local(): lax.psum_scatter(d_w_up, ('dp', 'ctx'), scatter_dimension=0, tiled=True)  162 us
    reduce_scatter x1, waiting for transfers between devices, local(): lax.psum_scatter(d_w_gate, ('dp', 'ctx'), scatter_dimension=0, tiled=True)  160 us
    reduce_scatter x1, waiting for transfers between devices, local(): lax.psum_scatter(d_w_value, ('dp', 'ctx'), scatter_dimension=0, tiled=True)  150 us
    reduce_scatter x1, waiting for transfers between devices, local(): lax.psum_scatter(d_w_key, ('dp', 'ctx'), scatter_dimension=0, tiled=True)  150 us
    reduce_scatter x1, waiting for transfers between devices, local(): lax.psum_scatter(d_w_query, ('dp', 'ctx'), scatter_dimension=0, tiled=True)  116 us
    dynamic_update_slice x4, local copies, waits for them, and re-layouts, local(): lax.map(attend_backward, (q_low, keys_all, values_all, grad_mix, log_tota...  92.5 us
  transfers between devices with their start and end apart: 18, of which 18 were waited for; matrix products, arithmetic and copies ran while one was open for 11% of the time, Pallas kernels for 0%

commit v1 on v0

--- a/solution.py
+++ b/solution.py
@@ -1,6 +1,11 @@
+import functools
+import math
+
 import jax
 import jax.numpy as jnp
 from jax import lax
+from jax.experimental import pallas as pl
+from jax.experimental.pallas import tpu as pltpu
 from jax.sharding import PartitionSpec as P
 
 D = 1024
@@ -268,6 +273,570 @@
     )
 
 
+AXES = ("dp", "ctx")
+SCALE = DH ** (-0.5)
+LOG2E = math.log2(math.e)
+NEG = -1e30
+BF = jnp.bfloat16
+F32 = jnp.float32
+
+
+class Place:
+    def __init__(self, dp_size, ctx_size):
+        self.count = dp_size * ctx_size
+        self.z_size = ctx_size
+        dp = lax.axis_index("dp")
+        self.z = lax.axis_index("ctx")
+        self.c = dp % 2
+        self.x = (dp // 2) % 2
+        self.y = dp // 4
+
+    def split(self, flat):
+        z, dp = flat % self.z_size, flat // self.z_size
+        return dp // 4, (dp // 2) % 2, dp % 2, z
+
+    def join(self, y, x, c, z):
+        return ((y * 2 + x) * 2 + c) * self.z_size + z
+
+    def move(self, values, target):
+        perm = []
+        for flat in range(self.count):
+            perm.append((flat, self.join(*target(*self.split(flat)))))
+        return lax.ppermute(values, AXES, perm)
+
+    def swap(self, values, axis):
+        return self.move(
+            values,
+            lambda y, x, c, z: (
+                1 - y if axis == "y" else y,
+                1 - x if axis == "x" else x,
+                1 - c if axis == "c" else c,
+                z,
+            ),
+        )
+
+    def shift(self, values, step):
+        return self.move(values, lambda y, x, c, z: (y, x, c, (z + step) % self.z_size))
+
+
+def after(values, *others):
+    return lax.optimization_barrier((values,) + tuple(others))[0]
+
+
+STRETCHES = ((0, 3), (1, 2))
+CORE_OF = (0, 1, 1, 0)
+RANK_OF = (0, 0, 1, 1)
+
+
+def rank_here(place):
+    return jnp.asarray(RANK_OF, jnp.int32)[place.z]
+
+
+def to_sequences(place, values):
+    parts = []
+    rank = rank_here(place)
+    for m in range(2):
+        chosen = lax.dynamic_index_in_dim(values, (rank + m) % 2, 0, keepdims=False)
+        parts.append(
+            place.move(
+                chosen, lambda y, x, c, z: (y, x, CORE_OF[z], 2 * c + (RANK_OF[z] + m) % 2)
+            )
+        )
+    first, second = parts
+    even = place.z % 2 == 0
+    return jnp.concatenate(
+        [jnp.where(even, first, second), jnp.where(even, second, first)], axis=0
+    )
+
+
+def from_sequences(place, values):
+    parts = []
+    for m in range(2):
+        chosen = lax.dynamic_index_in_dim(values, (m + place.z) % 2, 0, keepdims=False)
+        parts.append(
+            place.move(
+                chosen,
+                lambda y, x, c, z: (y, x, z // 2, STRETCHES[c][(m + z) % 2]),
+            )
+        )
+    first, second = parts
+    even = rank_here(place) == 0
+    return jnp.stack([jnp.where(even, first, second), jnp.where(even, second, first)])
+
+
+def gather_z(place, shard):
+    pieces = [shard] + [place.shift(shard, k) for k in range(1, place.z_size)]
+    return jnp.stack(pieces)
+
+
+def gather_rest(place, stacked, first_axis, second_axis):
+    both = jnp.stack([stacked, place.swap(stacked, first_axis)])
+    other = place.swap(both, second_axis)
+    return both, other, place.swap(both, "c"), place.swap(other, "c")
+
+
+def assemble(place, quarters, second_axis, widths):
+    z_size, rows, total = place.z_size, quarters[0].shape[2], quarters[0].shape[3]
+    first_is_x = second_axis == "y"
+    here = jnp.stack(
+        [place.x if first_is_x else place.y, place.y if first_is_x else place.x, place.c, place.z]
+    ).astype(jnp.int32)
+
+    def kernel(here_ref, near, far, near_core, far_core, *outs):
+        second, core = here_ref[1], here_ref[2]
+        for ref, from_second, from_core in (
+            (near, 0, 0),
+            (far, 1, 0),
+            (near_core, 0, 1),
+            (far_core, 1, 1),
+        ):
+            at_second = lax.rem(second + from_second, 2)
+            at_core = lax.rem(core + from_core, 2)
+            start = 0
+            for out, width in zip(outs, widths):
+                block = ref[0, 0, :, start : start + width]
+                if first_is_x:
+                    out[at_second, 0, at_core, 0] = block
+                else:
+                    out[0, at_second, at_core, 0] = block
+                start += width
+
+    def in_map(i, k, here_ref):
+        return (i, k, 0, 0)
+
+    def out_map(i, k, here_ref):
+        first = lax.rem(here_ref[0] + i, 2)
+        z = lax.rem(here_ref[3] + z_size - k, z_size)
+        return (0, first, 0, z, 0, 0) if first_is_x else (first, 0, 0, z, 0, 0)
+
+    def out_block(width):
+        return (2, 1, 2, 1, rows, width) if first_is_x else (1, 2, 2, 1, rows, width)
+
+    outs = pl.pallas_call(
+        kernel,
+        grid_spec=pltpu.PrefetchScalarGridSpec(
+            num_scalar_prefetch=1,
+            grid=(2, z_size),
+            in_specs=[pl.BlockSpec((1, 1, rows, total), in_map)] * 4,
+            out_specs=[pl.BlockSpec(out_block(width), out_map) for width in widths],
+        ),
+        out_shape=[
+            jax.ShapeDtypeStruct((2, 2, 2, z_size, rows, width), BF) for width in widths
+        ],
+        compiler_params=pltpu.CompilerParams(vmem_limit_bytes=32 * 2**20),
+        cost_estimate=pl.CostEstimate(
+            flops=0, bytes_accessed=2 * 8 * z_size * rows * total * 2, transcendentals=0
+        ),
+        name="assemble",
+    )(here, *quarters)
+    return [out.reshape(8 * z_size * rows, out.shape[-1]) for out in outs]
+
+
+def add_low(left, right):
+    return (left.astype(F32) + right.astype(F32)).astype(BF)
+
+
+def pick(values, index, axis):
+    return lax.dynamic_index_in_dim(values, index, axis, keepdims=False)
+
+
+def reduce_rows(place, grad, first_axis):
+    rows, width = grad.shape[0] // place.count, grad.shape[1]
+    parts = grad.reshape(2, 2, 2, place.z_size, rows, width)
+    parts = add_low(pick(parts, place.c, 2), place.swap(pick(parts, 1 - place.c, 2), "c"))
+    if first_axis == "y":
+        steps = (("y", place.y, 0), ("x", place.x, 0))
+    else:
+        steps = (("x", place.x, 1), ("y", place.y, 0))
+    for axis, index, dim in steps:
+        received = place.swap(pick(parts, 1 - index, dim), axis)
+        parts = add_low(pick(parts, index, dim), received)
+    total = pick(parts, place.z, 0).astype(F32)
+    for k in range(1, place.z_size):
+        sent = pick(parts, (place.z + k) % place.z_size, 0)
+        total = total + place.shift(sent, k).astype(F32)
+    return total
+
+
+def head_factor(values):
+    return lax.rsqrt(jnp.mean(values * values, axis=-1, keepdims=True) + norm_eps)
+
+
+def head_back(values, gain, upstream):
+    factor = head_factor(values)
+    weighted = upstream * gain
+    gain_grad = jnp.sum(upstream * values * factor, axis=0, keepdims=True)
+    inner_mean = jnp.mean(weighted * values, axis=-1, keepdims=True)
+    return gain_grad, factor * weighted - values * factor * factor * factor * inner_mean
+
+
+def turn(values, cosine, sine):
+    return values * cosine + pltpu.roll(values, DH // 2, 1) * sine
+
+
+def prepare_kv(kv_proj, gain, cosine, sine):
+    rows = kv_proj.shape[0]
+
+    def kernel(k_ref, v_ref, gain_ref, cos_ref, sin_ref, out_ref):
+        values = k_ref[...]
+        normed = values * head_factor(values) * gain_ref[...]
+        out_ref[0] = turn(normed, cos_ref[...], sin_ref[...]).astype(BF)
+        out_ref[1] = v_ref[...].astype(BF)
+
+    whole = lambda shape: pl.BlockSpec(shape, lambda h: (0, 0))
+    return pl.pallas_call(
+        kernel,
+        grid=(HK,),
+        in_specs=[
+            pl.BlockSpec((rows, DH), lambda h: (0, h)),
+            pl.BlockSpec((rows, DH), lambda h: (0, HK + h)),
+            whole((1, DH)),
+            whole((rows, DH)),
+            whole((rows, DH)),
+        ],
+        out_specs=pl.BlockSpec((2, rows, DH), lambda h: (0, 0, h)),
+        out_shape=jax.ShapeDtypeStruct((2, rows, HK * DH), BF),
+        cost_estimate=pl.CostEstimate(
+            flops=10 * rows * HK * DH, bytes_accessed=12 * rows * HK * DH, transcendentals=0
+        ),
+        name="prepare_kv",
+    )(kv_proj, kv_proj, gain, cosine, sine)
+
+
+def finish_kv(kv_proj, own, received, gain, cosine, sine):
+    rows = kv_proj.shape[0]
+
+    def kernel(k_ref, own_ref, other_ref, gain_ref, cos_ref, sin_ref, out_ref, gain_out):
+        @pl.when(pl.program_id(0) == 0)
+        def _():
+            gain_out[...] = jnp.zeros_like(gain_out)
+
+        grad_k = own_ref[0] + other_ref[0].astype(F32)
+        grad_kn = turn(grad_k, cos_ref[...], -sin_ref[...])
+        gain_grad, grad_kp = head_back(k_ref[...], gain_ref[...], grad_kn)
+        gain_out[...] += gain_grad
+        out_ref[0] = grad_kp.astype(BF)
+        out_ref[1] = (own_ref[1] + other_ref[1].astype(F32)).astype(BF)
+
+    whole = lambda shape: pl.BlockSpec(shape, lambda h: (0, 0))
+    pair = pl.BlockSpec((2, rows, DH), lambda h: (0, 0, h))
+    return pl.pallas_call(
+        kernel,
+        grid=(HK,),
+        in_specs=[
+            pl.BlockSpec((rows, DH), lambda h: (0, h)),
+            pair,
+            pair,
+            whole((1, DH)),
+            whole((rows, DH)),
+            whole((rows, DH)),
+        ],
+        out_specs=[pair, whole((1, DH))],
+        out_shape=[
+            jax.ShapeDtypeStruct((2, rows, HK * DH), BF),
+            jax.ShapeDtypeStruct((1, DH), F32),
+        ],
+        cost_estimate=pl.CostEstimate(
+            flops=30 * rows * HK * DH, bytes_accessed=20 * rows * HK * DH, transcendentals=0
+        ),
+        name="finish_kv",
+    )(kv_proj, own, received, gain, cosine, sine)
+
+
+def interleave(own, other):
+    half = own.shape[0] // 2
+    return jnp.concatenate([own[:half], other[:half], own[half:], other[half:]], axis=0)
+
+
+def fill_bias(q_ref, k_ref, bias_ref):
+    bias_ref[...] = jnp.where(
+        (k_ref[:, 0:1] <= q_ref[0:1, :]) & (k_ref[:, 1:2] == q_ref[1:2, :]), 0.0, NEG
+    ).astype(F32)
+
+
+NT = (((1,), (1,)), ((), ()))
+NN = (((1,), (0,)), ((), ()))
+
+
+def dot32(left, right, dims):
+    return lax.dot_general(left, right, dims, preferred_element_type=F32)
+
+
+def attend_fwd(q_proj, own_kv, other_kv, gain, cosine, sine, q_codes, k_codes):
+    rows = q_proj.shape[0]
+    half = rows // 2
+    keys_n = 2 * rows
+
+    def kernel(
+        q_ref, own_ref, other_ref, gain_ref, cos_ref, sin_ref, qc_ref, kc_ref,
+        mix_ref, q_low_ref, total_ref, bias_ref,
+    ):
+        @pl.when(pl.program_id(0) == 0)
+        def _():
+            fill_bias(qc_ref, kc_ref, bias_ref)
+
+        heads = []
+        for g in range(2):
+            values = q_ref[:, g * DH : (g + 1) * DH]
+            normed = values * head_factor(values) * gain_ref[...]
+            low = turn(normed, cos_ref[...], sin_ref[...]).astype(BF)
+            q_low_ref[:, g * DH : (g + 1) * DH] = low
+            heads.append(low)
+        keys = interleave(own_ref[0], other_ref[0])
+        values_t = interleave(own_ref[1], other_ref[1]).T
+        for part in range(2):
+            span = slice(part * half, (part + 1) * half)
+            count = keys_n if part else rows
+            queries = jnp.concatenate([heads[0][span], heads[1][span]], axis=0)
+            bias = bias_ref[:count, span]
+            scores = dot32(keys[:count], queries, NT) * (SCALE * LOG2E) + jnp.concatenate(
+                [bias, bias], axis=1
+            )
+            row_max = jnp.max(scores, axis=0, keepdims=True)
+            weights = jnp.exp2(scores - row_max)
+            row_total = jnp.sum(weights, axis=0, keepdims=True)
+            mix_t = dot32(values_t[:, :count], weights.astype(BF), NN) / row_total
+            mix = mix_t.T.astype(BF)
+            mix_ref[span, :DH] = mix[:half]
+            mix_ref[span, DH:] = mix[half:]
+            total_ref[0, part : part + 1, :] = row_max + jnp.log2(row_total)
+
+    whole = lambda shape: pl.BlockSpec(shape, lambda h: (0, 0))
+    pair = pl.BlockSpec((2, rows, DH), lambda h: (0, 0, h))
+    wide = pl.BlockSpec((rows, 2 * DH), lambda h: (0, h))
+    return pl.pallas_call(
+        kernel,
+        grid=(HK,),
+        in_specs=[
+            wide, pair, pair, whole((1, DH)), whole((rows, DH)), whole((rows, DH)),
+            whole((2, rows)), whole((keys_n, 2)),
+        ],
+        out_specs=[wide, wide, pl.BlockSpec((1, 2, rows), lambda h: (h, 0, 0))],
+        out_shape=[
+            jax.ShapeDtypeStruct((rows, HQ * DH), BF),
+            jax.ShapeDtypeStruct((rows, HQ * DH), BF),
+            jax.ShapeDtypeStruct((HK, 2, rows), F32),
+        ],
+        scratch_shapes=[pltpu.VMEM((keys_n, rows), F32)],
+        compiler_params=pltpu.CompilerParams(vmem_limit_bytes=48 * 2**20),
+        cost_estimate=pl.CostEstimate(
+            flops=HK * 2 * 2 * rows * 3 * rows * DH,
+            bytes_accessed=16 * 2**20,
+            transcendentals=HK * rows * 3 * rows,
+        ),
+        name="attend_fwd",
+    )(q_proj, own_kv, other_kv, gain, cosine, sine, q_codes, k_codes)
+
+
+def attend_bwd(
+    q_proj, q_low, own_kv, other_kv, grad_mix, totals, gain, cosine, sine, q_codes, k_codes
+):
+    rows = q_proj.shape[0]
+    half = rows // 2
+    keys_n = 2 * rows
+
+    def kernel(
+        q_ref, q_low_ref, own_ref, other_ref, grad_ref, total_ref, gain_ref, cos_ref, sin_ref,
+        qc_ref, kc_ref, grad_q_ref, grad_own_ref, grad_other_ref, gain_out, bias_ref,
+    ):
+        @pl.when(pl.program_id(0) == 0)
+        def _():
+            fill_bias(qc_ref, kc_ref, bias_ref)
+            gain_out[...] = jnp.zeros_like(gain_out)
+
+        keys = interleave(own_ref[0], other_ref[0])
+        keys_t = keys.T
+        values = interleave(own_ref[1], other_ref[1])
+        parts_q, parts_k, parts_v = [], [], []
+        for part in range(2):
+            span = slice(part * half, (part + 1) * half)
+            count = keys_n if part else rows
+            queries = jnp.concatenate([q_low_ref[span, :DH], q_low_ref[span, DH:]], axis=0)
+            grads = jnp.concatenate([grad_ref[span, :DH], grad_ref[span, DH:]], axis=0)
+            bias = bias_ref[:count, span]
+            scores = dot32(keys[:count], queries, NT) * (SCALE * LOG2E) + jnp.concatenate(
+                [bias, bias], axis=1
+            )
+            probs = jnp.exp2(scores - total_ref[0, part : part + 1, :])
+            grad_probs = dot32(values[:count], grads, NT)
+            product = probs * grad_probs
+            center = jnp.sum(product, axis=0, keepdims=True)
+            grad_scores = (product - probs * center).astype(BF)
+            parts_v.append(dot32(probs.astype(BF), grads, NN))
+            parts_k.append(dot32(grad_scores, queries, NN) * SCALE)
+            parts_q.append(dot32(keys_t[:, :count], grad_scores, NN).T * SCALE)
+        for slot, parts in ((0, parts_k), (1, parts_v)):
+            low_part, high_part = parts
+            both = high_part[:rows] + low_part
+            grad_own_ref[slot, :half] = both[:half]
+            grad_other_ref[slot, :half] = both[half:].astype(BF)
+            grad_own_ref[slot, half:] = high_part[rows : rows + half]
+            grad_other_ref[slot, half:] = high_part[rows + half :].astype(BF)
+        gain_total = gain_out[...]
+        for g in range(2):
+            grad_q = jnp.concatenate(
+                [parts_q[0][g * half : (g + 1) * half], parts_q[1][g * half : (g + 1) * half]],
+                axis=0,
+            )
+            grad_qn = turn(grad_q, cos_ref[...], -sin_ref[...])
+            gain_grad, grad_qp = head_back(
+                q_ref[:, g * DH : (g + 1) * DH], gain_ref[...], grad_qn
+            )
+            gain_total += gain_grad
+            grad_q_ref[:, g * DH : (g + 1) * DH] = grad_qp.astype(BF)
+        gain_out[...] = gain_total
+
+    whole = lambda shape: pl.BlockSpec(shape, lambda h: (0, 0))
+    pair = pl.BlockSpec((2, rows, DH), lambda h: (0, 0, h))
+    wide = pl.BlockSpec((rows, 2 * DH), lambda h: (0, h))
+    return pl.pallas_call(
+        kernel,
+        grid=(HK,),
+        in_specs=[
+            wide, wide, pair, pair, wide, pl.BlockSpec((1, 2, rows), lambda h: (h, 0, 0)),
+            whole((1, DH)), whole((rows, DH)), whole((rows, DH)),
+            whole((2, rows)), whole((keys_n, 2)),
+        ],
+        out_specs=[wide, pair, pair, whole((1, DH))],
+        out_shape=[
+            jax.ShapeDtypeStruct((rows, HQ * DH), BF),
+            jax.ShapeDtypeStruct((2, rows, HK * DH), F32),
+            jax.ShapeDtypeStruct((2, rows, HK * DH), BF),
+            jax.ShapeDtypeStruct((1, DH), F32),
+        ],
+        scratch_shapes=[pltpu.VMEM((keys_n, rows), F32)],
+        compiler_params=pltpu.CompilerParams(vmem_limit_bytes=56 * 2**20),
+        cost_estimate=pl.CostEstimate(
+            flops=HK * 5 * 2 * rows * 3 * rows * DH,
+            bytes_accessed=24 * 2**20,
+            transcendentals=HK * rows * 3 * rows,
+        ),
+        name="attend_bwd",
+    )(q_proj, q_low, own_kv, other_kv, grad_mix, totals, gain, cosine, sine, q_codes, k_codes)
+
+
+def mm(left, right, dims):
+    return jnp.einsum(dims, left, right, preferred_element_type=F32)
+
+
+def chip_local(
+    dp_size, ctx_size,
+    tokens, segments, positions, attn_gain, w_query, w_key, w_value, w_out, qk_gain, mlp_gain,
+    w_gate, w_up, w_down, cotangent,
+):
+    place = Place(dp_size, ctx_size)
+    _, stretch, _ = tokens.shape
+    rows = 2 * stretch
+    spread = lambda gain: jnp.broadcast_to(gain[:, None], (gain.shape[0], 128))
+
+    z_kv = gather_z(place, jnp.concatenate([w_key, w_value, spread(attn_gain)], axis=1))
+    z_q = gather_z(place, w_query)
+    seq_tokens = to_sequences(place, after(tokens, z_kv, z_q))
+    seq_positions = to_sequences(place, positions)
+    other_segments = place.swap(segments, "c")
+    z_out = gather_z(place, after(w_out, seq_tokens))
+    z_gate = gather_z(place, after(w_gate, z_out))
+    z_up = gather_z(place, after(jnp.concatenate([w_up, spread(mlp_gain)], axis=1), z_out))
+    seq_cotangent = to_sequences(place, after(cotangent, z_gate, z_up))
+    z_down = gather_z(place, after(w_down, seq_cotangent))
+
+    four_kv = gather_rest(place, z_kv, "y", "x")
+    four_q = gather_rest(place, z_q, "x", "y")
+    four_out = gather_rest(place, after(z_out, four_q[1]), "x", "y")
+    four_up = gather_rest(place, after(z_up, four_kv[1]), "y", "x")
+    four_gate = gather_rest(place, after(z_gate, four_out[1]), "x", "y")
+    four_down = gather_rest(place, after(z_down, four_up[1]), "y", "x")
+    kv_full, g_attn = assemble(place, four_kv, "x", (2 * HK * DH, 128))
+    (q_full,) = assemble(place, four_q, "y", (HQ * DH,))
+    (out_full,) = assemble(place, four_out, "y", (HQ * DH,))
+    up_full, g_mlp = assemble(place, four_up, "x", (w_up.shape[1], 128))
+    (gate_full,) = assemble(place, four_gate, "y", (w_gate.shape[1],))
+    (down_full,) = assemble(place, four_down, "x", (w_down.shape[1],))
+    g_attn = g_attn[:, 0].astype(F32)
+    g_mlp = g_mlp[:, 0].astype(F32)
+
+    segment_rows = jnp.where(place.z // 2 == place.c, segments, other_segments)
+    segment_row = pick(segment_rows, place.z % 2, 0)
+    within = jnp.arange(stretch, dtype=jnp.int32)
+    near = jnp.where(place.c == 0, 0, 1) * stretch + within
+    far = jnp.where(place.c == 0, 3, 2) * stretch + within
+    other_near = jnp.where(place.c == 0, 1, 0) * stretch + within
+    other_far = jnp.where(place.c == 0, 2, 3) * stretch + within
+    q_places = jnp.concatenate([near, far])
+    k_places = jnp.concatenate([near, other_near, far, other_far])
+    q_codes = jnp.stack([q_places, segment_row[q_places]])
+    k_codes = jnp.stack([k_places, segment_row[k_places]], axis=1)
+    inv_freq = rope_base ** (-2.0 * jnp.arange(DH // 2, dtype=F32) / DH)
+    angles = seq_positions.reshape(rows).astype(F32)[:, None] * inv_freq
+    cosine, sine = jnp.cos(angles), jnp.sin(angles)
+    cosine = jnp.concatenate([cosine, cosine], axis=1)
+    sine = jnp.concatenate([-sine, sine], axis=1)
+    gains_qk = qk_gain.astype(F32)
+    q_gain, k_gain = gains_qk[0:1], gains_qk[1:2]
+
+    resid_in = seq_tokens.reshape(rows, D).astype(F32)
+    normed_f, factor_in = norm_rows(resid_in, g_attn)
+    normed = normed_f.astype(BF)
+    kv_proj = mm(normed, kv_full, "td,dh->th")
+    own_kv = prepare_kv(kv_proj, k_gain, cosine, sine)
+    other_kv = place.swap(own_kv, "c")
+    q_proj = mm(normed, q_full, "td,dh->th")
+    attn_mix, q_low, totals = attend_fwd(
+        q_proj, own_kv, other_kv, q_gain, cosine, sine, q_codes, k_codes
+    )
+    hidden_in = resid_in + mm(attn_mix, out_full, "th,dh->td")
+    normed_mlp_f, factor_mlp = norm_rows(hidden_in, g_mlp)
+    normed_mlp = normed_mlp_f.astype(BF)
+    gated = mm(normed_mlp, gate_full, "td,df->tf")
+    upward = mm(normed_mlp, up_full, "td,df->tf")
+    sigmoid_gate = jax.nn.sigmoid(gated)
+    silu_gate = gated * sigmoid_gate
+    inner = (silu_gate * upward).astype(BF)
+    result = (hidden_in + mm(inner, down_full, "tf,df->td")).astype(BF)
+    layer_out = from_sequences(place, result.reshape(2, stretch, D))
+
+    grad_out = seq_cotangent.reshape(rows, D)
+    d_down = reduce_rows(place, mm(grad_out, inner, "td,tf->df").astype(BF), "x")
+    grad_inner = mm(grad_out, down_full, "td,df->tf")
+    grad_gate = (grad_inner * upward * sigmoid_gate * (1.0 + gated * (1.0 - sigmoid_gate))).astype(BF)
+    grad_up = (grad_inner * silu_gate).astype(BF)
+    d_gate = reduce_rows(place, mm(normed_mlp, grad_gate, "td,tf->df").astype(BF), "y")
+    d_up = reduce_rows(place, mm(normed_mlp, grad_up, "td,tf->df").astype(BF), "x")
+    grad_normed_mlp = mm(grad_gate, gate_full, "tf,df->td") + mm(grad_up, up_full, "tf,df->td")
+    mlp_gain_part, grad_resid_mlp = norm_back(hidden_in, factor_mlp, g_mlp, grad_normed_mlp)
+    grad_hidden = grad_out.astype(F32) + grad_resid_mlp
+
+    grad_attn = grad_hidden.astype(BF)
+    grad_mix = mm(grad_attn, out_full, "td,dh->th").astype(BF)
+    d_out = reduce_rows(place, mm(grad_attn, attn_mix, "td,th->dh").astype(BF), "y")
+    grad_q_low, own_grad, other_grad, q_gain_part = attend_bwd(
+        q_proj, q_low, own_kv, other_kv, grad_mix, totals, q_gain, cosine, sine, q_codes, k_codes
+    )
+    received = place.swap(other_grad, "c")
+    grad_kv_low, k_gain_part = finish_kv(kv_proj, own_grad, received, k_gain, cosine, sine)
+    grad_kv_low = jnp.concatenate([grad_kv_low[0], grad_kv_low[1]], axis=1)
+    d_query = reduce_rows(place, mm(normed, grad_q_low, "td,th->dh").astype(BF), "y")
+    d_kv = reduce_rows(place, mm(normed, grad_kv_low, "td,th->dh").astype(BF), "x")
+    grad_normed = mm(grad_q_low, q_full, "th,dh->td") + mm(grad_kv_low, kv_full, "th,dh->td")
+    attn_gain_part, grad_resid_attn = norm_back(resid_in, factor_in, g_attn, grad_normed)
+    d_seq = (grad_hidden + grad_resid_attn).astype(BF)
+    d_tokens = from_sequences(place, d_seq.reshape(2, stretch, D)).astype(F32)
+
+    small = jnp.concatenate(
+        [attn_gain_part, mlp_gain_part, q_gain_part.reshape(DH), k_gain_part.reshape(DH)]
+    )
+    small = jnp.sum(lax.all_gather(small, AXES, axis=0, tiled=False), axis=0)
+    flat = lax.axis_index("dp") * ctx_size + lax.axis_index("ctx")
+    own = D // place.count
+    d_attn_gain = lax.dynamic_slice_in_dim(small, flat * own, own)
+    d_mlp_gain = lax.dynamic_slice_in_dim(small, D + flat * own, own)
+    d_qk_gain = small[2 * D :].reshape(2, DH)
+    return (
+        layer_out, d_tokens, d_attn_gain, d_query, d_kv[:, : HK * DH], d_kv[:, HK * DH :], d_out,
+        d_qk_gain, d_mlp_gain, d_gate, d_up, d_down,
+    )
+
+
 def solution(mesh):
     in_specs = (
         P("dp", "ctx", None),
@@ -299,4 +868,8 @@
         P(("dp", "ctx"), None),
         P(("dp", "ctx"), None),
     )
-    return jax.shard_map(local, mesh=mesh, in_specs=in_specs, out_specs=out_specs, check_vma=False)
+    dp_size, ctx_size = mesh.shape["dp"], mesh.shape["ctx"]
+    body = local
+    if dp_size == 8 and ctx_size == 4:
+        body = functools.partial(chip_local, dp_size, ctx_size)
+    return jax.shard_map(body, mesh=mesh, in_specs=in_specs, out_specs=out_specs, check_vma=False)

time: 2210 us -> 740 us (0.33)
  waiting for transfers between devices: 1610 us -> 227 us
  matrix products: 237 us -> 94.3 us
  starting transfers between devices: 1.28 us -> 134 us
  local copies, waits for them, and re-layouts: 174 us -> 55.7 us
  Pallas kernels: 0 us -> 88.5 us
    reduce_scatter x8 -> x0, waiting for transfers between devices: 995 us -> none  [the longest x1 186 us: local(): lax.psum_scatter(d_w_out, ('dp', 'ctx'), scatter_dimension=0, tiled=True)]
    all_gather x9 -> x0, waiting for transfers between devices: 444 us -> none  [the longest x1 80.7 us: local(): lax.all_gather(k_low, 'ctx', axis=1, tiled=True)]
    ppermute x0 -> x91, waiting for transfers between devices: none -> 227 us  [move(): return lax.ppermute(values, AXES, perm)]
    unnamed x19 -> x0, waiting for transfers between devices: 167 us -> none
    dot_general x35 -> x18, matrix products: 237 us -> 94.3 us  [mm(): return jnp.einsum(dims, left, right, preferred_element_type=F32)]
    ppermute x0 -> x91, starting transfers between devices: none -> 134 us  [move(): return lax.ppermute(values, AXES, perm)]
    dynamic_update_slice x8 -> x0, local copies, waits for them, and re-layouts: 95.8 us -> none  [the longest x4 92.5 us: local(): lax.map(attend_backward, (q_low, keys_all, values_all, grad_mix, log_tota...]
    pallas_call x0 -> x10, Pallas kernels: none -> 88.5 us  [the longest x6 29.8 us: assemble(): pl.pallas_call(kernel, grid_spec=pltpu.PrefetchScalarGridSpec(num_scalar_...]
  transfers between devices with their start and end apart: 18 -> 91, of which waited for: 18 -> 29; matrix products, arithmetic and copies ran while one was open for 11% -> 18% of each run, Pallas kernels for 0% -> 11%
where the time goes in v1:
time: 740 us; the launch traced here: 727 us
  waiting for transfers between devices  227 us (31%)
  starting transfers between devices  134 us (18%)
  matrix products  94.3 us (13%)
  Pallas kernels  88.5 us (12%)
  blocking collectives  72.2 us (10%)
  local copies, waits for them, and re-layouts  55.7 us (8%)
  other arithmetic  49.5 us (7%)
    ppermute x91, waiting for transfers between devices, move(): return lax.ppermute(values, AXES, perm)  227 us
    ppermute x91, starting transfers between devices, move(): return lax.ppermute(values, AXES, perm)  134 us
    dot_general x18, matrix products, mm(): return jnp.einsum(dims, left, right, preferred_element_type=F32)  94.3 us
    all_gather x1, blocking collectives, chip_local(): small = jnp.sum(lax.all_gather(small, AXES, axis=0, tiled=False), axis=0)  72.2 us
    pallas_call x6, Pallas kernels, assemble(): pl.pallas_call(kernel, grid_spec=pltpu.PrefetchScalarGridSpec(num_scalar_...  29.8 us
    pallas_call x1, Pallas kernels, attend_bwd(): pl.pallas_call(kernel, grid=(HK,), in_specs=[wide, wide, pair, pair, wide...  25.6 us
    unnamed x149, local copies, waits for them, and re-layouts  18.4 us
    pallas_call x1, Pallas kernels, attend_fwd(): pl.pallas_call(kernel, grid=(HK,), in_specs=[wide, pair, pair, whole((1,...  17.6 us
  transfers between devices with their start and end apart: 91, of which 29 were waited for; matrix products, arithmetic and copies ran while one was open for 18% of the time, Pallas kernels for 11%

profile of v1, /device:TPU:0, one launch (start us, length us, event | category | flops | bytes accessed | tf_op | source)
XLA Modules:
  0.0 726.9 jit_solution(8397775196366978292)
XLA Ops:
  15.7 11.8 %collective-permute-start.3 = (bf16[32,2048]{1,0:T(8,128)(2,1)}, bf16[32,2048]{1,0:T(8,128)(2,1)S(1)}, u32[]{:S(2)}, u32[]{:S(2)}) collective-permute-start(bf16[32,2048]{1,0:T(8,128)(2,1)} %param.23), channel_id=1, source_target_pairs={{0,1},{1,2},{2,3},{3,0},{4,5},{5,6},{6,7},{7,4},{8,9},{9,10},{10,1... | collective-permute-start | bytes 393224 | tf_op jit(solution)/shard_map/ppermute | solution.py:305
  46.9 5.4 collective-permute-start.29
  57.9 10.4 %collective-permute-start.17 = (s32[256]{0:T(256)S(1)}, s32[256]{0:T(256)S(1)}, u32[]{:S(2)}, u32[]{:S(2)}) collective-permute-start(s32[256]{0:T(256)S(1)} %bitcast.376), channel_id=1, source_target_pairs={{0,1},{1,5},{2,4},{3,0},{4,3},{5,7},{6,6},{7,2},{8,9},{9,13},{10,1... | collective-permute-start | bytes 3080 | tf_op jit(solution)/shard_map/ppermute | solution.py:305
  80.7 15.7 %collective-permute-done.13.far = bf16[2,4,32,2048]{3,2,1,0:T(8,128)(2,1)} collective-permute-done((bf16[2,4,32,2048]{3,2,1,0:T(8,128)(2,1)}, bf16[2,4,32,2048]{3,2,1,0:T(8,128)(2,1)}, u32[]{:S(2)}, u32[]{:S(2)}) %collective-permute-start.13) | collective-permute-done | bytes 1048608 | tf_op jit(solution)/shard_map/ppermute | solution.py:305
  97.3 14.3 %collective-permute-done.30 = bf16[4,32,3200]{2,1,0:T(8,128)(2,1)S(1)} collective-permute-done((bf16[4,32,3200]{2,1,0:T(8,128)(2,1)S(1)}, bf16[4,32,3200]{2,1,0:T(8,128)(2,1)S(1)}, u32[]{:S(2)}, u32[]{:S(2)}) %collective-permute-start.30) | collective-permute-done | bytes 819232 | tf_op jit(solution)/shard_map/ppermute | solution.py:305
  116.5 13.1 %collective-permute-done.35 = bf16[32,3072]{1,0:T(8,128)(2,1)S(1)} collective-permute-done((bf16[32,3072]{1,0:T(8,128)(2,1)S(1)}, bf16[32,3072]{1,0:T(8,128)(2,1)S(1)}, u32[]{:S(2)}, u32[]{:S(2)}) %collective-permute-start.35) | collective-permute-done | bytes 196640 | tf_op jit(solution)/shard_map/ppermute | solution.py:305
  136.8 8.0 %collective-permute-done.7 = bf16[256,1024]{1,0:T(8,128)(2,1)S(1)} collective-permute-done((bf16[256,1024]{1,0:T(8,128)(2,1)S(1)}, bf16[256,1024]{1,0:T(8,128)(2,1)S(1)}, u32[]{:S(2)}, u32[]{:S(2)}) %collective-permute-start.7) | collective-permute-done | bytes 524320 | tf_op jit(solution)/shard_map/ppermute | solution.py:305
  161.8 6.8 fusion.55.k_ref.v_ref
  168.5 7.0 prepare_kv.1.own_ref
  196.4 5.5 assemble.7
  208.5 5.5 assemble.8
  214.2 17.6 %attend_fwd.1 = (bf16[512,2048]{1,0:T(8,128)(2,1)S(1)}, bf16[512,2048]{1,0:T(8,128)(2,1)S(1)}, f32[8,2,512]{2,1,0:T(2,128)S(1)}) custom-call(f32[512,2048]{1,0:T(8,128)} %fusion.57.q_ref, bf16[2,512,1024]{2,1,0:T(8,128)(2,1)} %prepare_kv.1.own_ref, bf16[2,512,1024]{2,1,0:T(8,128)(2,1)} %collective-permute-done.18.other_ref, ...), custom_call_target="tpu_custom_call" | custom-call | flops 3221225472 | bytes 16777216 | tf_op jit(solution)/shard_map/attend_fwd/pallas_call | solution.py:607
  231.8 5.7 multiply_reduce_fusion.2
  248.4 8.4 %fusion.62 = f32[512,3072]{1,0:T(8,128)} fusion(bf16[512,1024]{1,0:T(8,128)(2,1)S(1)} %multiply_convert_fusion.3, bf16[1024,3072]{1,0:T(8,128)(2,1)} %bitcast.303), kind=kOutput, calls=%fused_computation.225 | convolution fusion | flops 3221225472 | bytes 13631488 | tf_op jit(solution)/shard_map/td,df->tf/dot_general | solution.py:719
  256.8 6.2 assemble.10
  263.0 5.8 assemble.11
  274.2 11.5 %multiply_convert_fusion.1 = (bf16[512,3072]{1,0:T(8,128)(2,1)}, bf16[512,3072]{1,0:T(8,128)(2,1)}, bf16[512,3072]{1,0:T(8,128)(2,1)}) fusion(f32[512,3072]{1,0:T(8,128)} %fusion.52, f32[512,3072]{1,0:T(8,128)} %fusion.62, bf16[512,1024]{1,0:T(8,128)(2,1)S(1)} %copy-done.47, bf16[1024,3072]{1,0:T(8,128)(2,1)S(1)} %bitcast.295), kind=kOutput, calls=%fused_computation.9 | convolution fusion | flops 3244818432 | bytes 29360128 | tf_op jit(solution)/shard_map/td,df->tf/dot_general | solution.py:719
  285.7 5.5 fusion.63
  291.2 5.9 multiply_reduce_fusion
  329.3 25.6 %attend_bwd.1 = (bf16[512,2048]{1,0:T(8,128)(2,1)}, f32[2,512,1024]{2,1,0:T(8,128)}, bf16[2,512,1024]{2,1,0:T(8,128)(2,1)}, f32[1,128]{1,0:T(1,128)}) custom-call(f32[512,2048]{1,0:T(8,128)} %fusion.57.q_ref, bf16[512,2048]{1,0:T(8,128)(2,1)} %copy-done.14, bf16[2,512,1024]{2,1,0:T(8,128)(2,1)} %prepare_kv.1.own_ref, ...), custom_call_target="tpu_custom_call" | custom-call | flops 8053063680 | bytes 25165824 | tf_op jit(solution)/shard_map/attend_bwd/pallas_call | solution.py:692
  367.8 5.9 convolution_convert_fusion.2
  383.7 8.6 %finish_kv.1 = (bf16[2,512,1024]{2,1,0:T(8,128)(2,1)}, f32[1,128]{1,0:T(1,128)}) custom-call(f32[512,2048]{1,0:T(8,128)} %fusion.55.k_ref.v_ref, f32[2,512,1024]{2,1,0:T(8,128)} %get-tuple-element.53.own_ref, bf16[2,512,1024]{2,1,0:T(8,128)(2,1)} %collective-permute-done.52.other_ref, f32[1,128]{1,0:T(1,128)} %get-tuple-element.125.gain_ref, ...), custom_call_target="tpu_custom_call" | custom-call | flops 15728640 | bytes 10485760 | tf_op jit(solution)/shard_map/finish_kv/pallas_call | solution.py:523
  418.9 72.2 %all-gather.1 = f32[32,1,2304]{2,1,0:T(1,128)S(1)} all-gather(f32[1,1,2304]{2,1,0:T(1,128)S(1)} %reshape.404), channel_id=2, replica_groups=mesh['dp'=8,'ctx'=4] {'dp','ctx'}, dimensions={0}, use_global_device_ids=true | all-gather | bytes 304128 | tf_op jit(solution)/shard_map/all_gather | solution.py:828
  506.2 18.7 %collective-permute-done.68 = bf16[2,4,32,2048]{3,2,1,0:T(8,128)(2,1)S(1)} collective-permute-done((bf16[2,4,32,2048]{3,2,1,0:T(8,128)(2,1)S(1)}, bf16[2,4,32,2048]{3,2,1,0:T(8,128)(2,1)S(1)}, u32[]{:S(2)}, u32[]{:S(2)}) %collective-permute-start.68) | collective-permute-done | bytes 1048608 | tf_op jit(solution)/shard_map/ppermute | solution.py:305
  540.4 9.3 %collective-permute-done.69 = bf16[4,32,2048]{2,1,0:T(8,128)(2,1)S(1)} collective-permute-done((bf16[4,32,2048]{2,1,0:T(8,128)(2,1)}, bf16[4,32,2048]{2,1,0:T(8,128)(2,1)S(1)}, u32[]{:S(2)}, u32[]{:S(2)}) %collective-permute-start.69) | collective-permute-done | bytes 524320 | tf_op jit(solution)/shard_map/ppermute | solution.py:305
  569.5 26.9 %collective-permute-done.80 = bf16[2,4,32,3072]{3,2,1,0:T(8,128)(2,1)S(1)} collective-permute-done((bf16[2,4,32,3072]{3,2,1,0:T(8,128)(2,1)S(1)}, bf16[2,4,32,3072]{3,2,1,0:T(8,128)(2,1)S(1)}, u32[]{:S(2)}, u32[]{:S(2)}) %collective-permute-start.80) | collective-permute-done | bytes 1572896 | tf_op jit(solution)/shard_map/ppermute | solution.py:305
  597.7 32.4 %collective-permute-done.86 = bf16[2,4,32,3072]{3,2,1,0:T(8,128)(2,1)S(1)} collective-permute-done((bf16[2,4,32,3072]{3,2,1,0:T(8,128)(2,1)S(1)}, bf16[2,4,32,3072]{3,2,1,0:T(8,128)(2,1)S(1)}, u32[]{:S(2)}, u32[]{:S(2)}) %collective-permute-start.86) | collective-permute-done | bytes 1572896 | tf_op jit(solution)/shard_map/ppermute | solution.py:305
  631.4 21.1 %collective-permute-done.62 = bf16[2,4,32,2048]{3,2,1,0:T(8,128)(2,1)S(1)} collective-permute-done((bf16[2,4,32,2048]{3,2,1,0:T(8,128)(2,1)S(1)}, bf16[2,4,32,2048]{3,2,1,0:T(8,128)(2,1)S(1)}, u32[]{:S(2)}, u32[]{:S(2)}) %collective-permute-start.62) | collective-permute-done | bytes 1048608 | tf_op jit(solution)/shard_map/ppermute | solution.py:305
  653.7 10.6 %collective-permute-done.75 = bf16[4,32,3072]{2,1,0:T(8,128)(2,1)S(1)} collective-permute-done((bf16[4,32,3072]{2,1,0:T(8,128)(2,1)S(1)}, bf16[4,32,3072]{2,1,0:T(8,128)(2,1)S(1)}, u32[]{:S(2)}, u32[]{:S(2)}) %collective-permute-start.75) | collective-permute-done | bytes 786464 | tf_op jit(solution)/shard_map/ppermute | solution.py:305
  675.1 14.1 %collective-permute-done.77 = bf16[32,3072]{1,0:T(8,128)(2,1)S(1)} collective-permute-done((bf16[32,3072]{1,0:T(8,128)(2,1)S(1)}, bf16[32,3072]{1,0:T(8,128)(2,1)S(1)}, u32[]{:S(2)}, u32[]{:S(2)}) %collective-permute-start.77) | collective-permute-done | bytes 196640 | tf_op jit(solution)/shard_map/ppermute | solution.py:305
  703.0 5.9 collective-permute-start.66
  714.3 7.8 %collective-permute-done.89 = bf16[32,3072]{1,0:T(8,128)(2,1)S(1)} collective-permute-done((bf16[32,3072]{1,0:T(8,128)(2,1)S(1)}, bf16[32,3072]{1,0:T(8,128)(2,1)S(1)}, u32[]{:S(2)}, u32[]{:S(2)}) %collective-permute-start.89) | collective-permute-done | bytes 196640 | tf_op jit(solution)/shard_map/ppermute | solution.py:305
  (449 shorter events, 291.7 us)
Async XLA Ops:
  0.7 33.5 %collective-permute-start.5 = (bf16[32,2048]{1,0:T(8,128)(2,1)}, bf16[32,2048]{1,0:T(8,128)(2,1)S(1)}, u32[]{:S(2)}, u32[]{:S(2)}) collective-permute-start(bf16[32,2048]{1,0:T(8,128)(2,1)} %param.23), channel_id=1, source_target_pairs={{0,3},{1,0},{2,1},{3,2},{4,7},{5,4},{6,5},{7,6},{8,11},{9,8},{10,9... | collective-permute-start | bytes 393224 | tf_op jit(solution)/shard_map/ppermute | solution.py:305
  45.0 32.1 %collective-permute-start.16 = (s32[256]{0:T(256)S(1)}, s32[256]{0:T(256)S(1)}, u32[]{:S(2)}, u32[]{:S(2)}) collective-permute-start(s32[256]{0:T(256)S(1)} %bitcast.377), channel_id=1, source_target_pairs={{0,0},{1,4},{2,5},{3,1},{4,2},{5,6},{6,7},{7,3},{8,8},{9,12},{10,1... | collective-permute-start | bytes 3080 | tf_op jit(solution)/shard_map/ppermute | solution.py:305
  69.8 42.4 %collective-permute-start.45 = (bf16[32,3072]{1,0:T(8,128)(2,1)S(1)}, bf16[32,3072]{1,0:T(8,128)(2,1)S(1)}, u32[]{:S(2)}, u32[]{:S(2)}) collective-permute-start(bf16[32,3072]{1,0:T(8,128)(2,1)S(1)} %copy-done.54), channel_id=1, source_target_pairs={{0,3},{1,0},{2,1},{3,2},{4,7},{5,4},{6,5},{7,6},{8,11},{9,8},{10,9... | collective-permute-start | bytes 589832 | tf_op jit(solution)/shard_map/ppermute | solution.py:305
  74.5 38.1 %collective-permute-start.44 = (bf16[32,3072]{1,0:T(8,128)(2,1)S(1)}, bf16[32,3072]{1,0:T(8,128)(2,1)S(1)}, u32[]{:S(2)}, u32[]{:S(2)}) collective-permute-start(bf16[32,3072]{1,0:T(8,128)(2,1)S(1)} %copy-done.54), channel_id=1, source_target_pairs={{0,2},{1,3},{2,0},{3,1},{4,6},{5,7},{6,4},{7,5},{8,10},{9,11},{10,... | collective-permute-start | bytes 589832 | tf_op jit(solution)/shard_map/ppermute | solution.py:305
  77.0 36.2 %collective-permute-start.43 = (bf16[32,3072]{1,0:T(8,128)(2,1)S(1)}, bf16[32,3072]{1,0:T(8,128)(2,1)S(1)}, u32[]{:S(2)}, u32[]{:S(2)}) collective-permute-start(bf16[32,3072]{1,0:T(8,128)(2,1)S(1)} %copy-done.54), channel_id=1, source_target_pairs={{0,1},{1,2},{2,3},{3,0},{4,5},{5,6},{6,7},{7,4},{8,9},{9,10},{10,1... | collective-permute-start | bytes 589832 | tf_op jit(solution)/shard_map/ppermute | solution.py:305
  77.4 34.2 %collective-permute-start.30 = (bf16[4,32,3200]{2,1,0:T(8,128)(2,1)S(1)}, bf16[4,32,3200]{2,1,0:T(8,128)(2,1)S(1)}, u32[]{:S(2)}, u32[]{:S(2)}) collective-permute-start(bf16[4,32,3200]{2,1,0:T(8,128)(2,1)S(1)} %pad_maximum_fusion.12), channel_id=1, source_target_pairs={{0,16},{1,17},{2,18},{3,19},{4,20},{5,21},{6,22},{7,23},{8,24},{9,... | collective-permute-start | bytes 2457608 | tf_op jit(solution)/shard_map/ppermute | solution.py:305
  114.0 46.2 %collective-permute-start.31 = (bf16[2,4,32,3200]{3,2,1,0:T(8,128)(2,1)S(1)}, bf16[2,4,32,3200]{3,2,1,0:T(8,128)(2,1)}, u32[]{:S(2)}, u32[]{:S(2)}) collective-permute-start(bf16[2,4,32,3200]{3,2,1,0:T(8,128)(2,1)S(1)} %pad_maximum_fusion.1.near), channel_id=1, source_target_pairs={{0,8},{1,9},{2,10},{3,11},{4,12},{5,13},{6,14},{7,15},{8,0},{9,1},... | collective-permute-start | bytes 4915208 | tf_op jit(solution)/shard_map/ppermute | solution.py:305
  175.5 38.6 %collective-permute-start.18 = (bf16[2,512,1024]{2,1,0:T(8,128)(2,1)}, bf16[2,512,1024]{2,1,0:T(8,128)(2,1)}, u32[]{:S(2)}, u32[]{:S(2)}) collective-permute-start(bf16[2,512,1024]{2,1,0:T(8,128)(2,1)} %prepare_kv.1.own_ref), channel_id=1, source_target_pairs={{0,4},{1,5},{2,6},{3,7},{4,0},{5,1},{6,2},{7,3},{8,12},{9,13},{10,... | collective-permute-start | bytes 6291464 | tf_op jit(solution)/shard_map/ppermute | solution.py:305
  191.0 46.5 %collective-permute-start.32 = (bf16[2,4,32,3200]{3,2,1,0:T(8,128)(2,1)S(1)}, bf16[2,4,32,3200]{3,2,1,0:T(8,128)(2,1)S(1)}, u32[]{:S(2)}, u32[]{:S(2)}) collective-permute-start(bf16[2,4,32,3200]{3,2,1,0:T(8,128)(2,1)S(1)} %pad_maximum_fusion.1.near), channel_id=1, source_target_pairs={{0,4},{1,5},{2,6},{3,7},{4,0},{5,1},{6,2},{7,3},{8,12},{9,13},{10,... | collective-permute-start | bytes 4915208 | tf_op jit(solution)/shard_map/ppermute | solution.py:305
  191.1 46.8 %collective-permute-start.38 = (bf16[2,4,32,3072]{3,2,1,0:T(8,128)(2,1)}, bf16[2,4,32,3072]{3,2,1,0:T(8,128)(2,1)}, u32[]{:S(2)}, u32[]{:S(2)}) collective-permute-start(bf16[2,4,32,3072]{3,2,1,0:T(8,128)(2,1)} %pad_maximum_fusion.2.near), channel_id=1, source_target_pairs={{0,16},{1,17},{2,18},{3,19},{4,20},{5,21},{6,22},{7,23},{8,24},{9,... | collective-permute-start | bytes 4718600 | tf_op jit(solution)/shard_map/ppermute | solution.py:305
  192.7 45.4 %collective-permute-start.47 = (bf16[2,4,32,3072]{3,2,1,0:T(8,128)(2,1)S(1)}, bf16[2,4,32,3072]{3,2,1,0:T(8,128)(2,1)}, u32[]{:S(2)}, u32[]{:S(2)}) collective-permute-start(bf16[2,4,32,3072]{3,2,1,0:T(8,128)(2,1)S(1)} %pad_maximum_fusion.3.near), channel_id=1, source_target_pairs={{0,8},{1,9},{2,10},{3,11},{4,12},{5,13},{6,14},{7,15},{8,0},{9,1},... | collective-permute-start | bytes 4718600 | tf_op jit(solution)/shard_map/ppermute | solution.py:305
  202.0 36.5 %collective-permute-start.33 = (bf16[2,4,32,3200]{3,2,1,0:T(8,128)(2,1)}, bf16[2,4,32,3200]{3,2,1,0:T(8,128)(2,1)S(1)}, u32[]{:S(2)}, u32[]{:S(2)}) collective-permute-start(bf16[2,4,32,3200]{3,2,1,0:T(8,128)(2,1)} %collective-permute-done.31.far), channel_id=1, source_target_pairs={{0,4},{1,5},{2,6},{3,7},{4,0},{5,1},{6,2},{7,3},{8,12},{9,13},{10,... | collective-permute-start | bytes 4915208 | tf_op jit(solution)/shard_map/ppermute | solution.py:305
  214.0 42.8 %collective-permute-start.39 = (bf16[2,4,32,3072]{3,2,1,0:T(8,128)(2,1)}, bf16[2,4,32,3072]{3,2,1,0:T(8,128)(2,1)}, u32[]{:S(2)}, u32[]{:S(2)}) collective-permute-start(bf16[2,4,32,3072]{3,2,1,0:T(8,128)(2,1)} %pad_maximum_fusion.2.near), channel_id=1, source_target_pairs={{0,4},{1,5},{2,6},{3,7},{4,0},{5,1},{6,2},{7,3},{8,12},{9,13},{10,... | collective-permute-start | bytes 4718600 | tf_op jit(solution)/shard_map/ppermute | solution.py:305
  321.5 59.4 %collective-permute-start.50 = (bf16[256,1024]{1,0:T(8,128)(2,1)}, bf16[256,1024]{1,0:T(8,128)(2,1)}, u32[]{:S(2)}, u32[]{:S(2)}) collective-permute-start(bf16[256,1024]{1,0:T(8,128)(2,1)} %get-tuple-element.83), channel_id=1, source_target_pairs={{0,0},{1,3},{2,4},{3,7},{4,1},{5,2},{6,5},{7,6},{8,8},{9,11},{10,1... | collective-permute-start | bytes 1572872 | tf_op jit(solution)/shard_map/ppermute | solution.py:305
  326.9 54.0 %collective-permute-start.51 = (bf16[256,1024]{1,0:T(8,128)(2,1)}, bf16[256,1024]{1,0:T(8,128)(2,1)}, u32[]{:S(2)}, u32[]{:S(2)}) collective-permute-start(bf16[256,1024]{1,0:T(8,128)(2,1)} %get-tuple-element.84), channel_id=1, source_target_pairs={{0,3},{1,0},{2,7},{3,4},{4,2},{5,1},{6,6},{7,5},{8,11},{9,8},{10,1... | collective-permute-start | bytes 1572872 | tf_op jit(solution)/shard_map/ppermute | solution.py:305
  362.2 46.5 %collective-permute-start.55 = (bf16[2,2,4,32,2048]{4,3,2,1,0:T(8,128)(2,1)}, bf16[2,2,4,32,2048]{4,3,2,1,0:T(8,128)(2,1)}, u32[]{:S(2)}, u32[]{:S(2)}) collective-permute-start(bf16[2,2,4,32,2048]{4,3,2,1,0:T(8,128)(2,1)} %dynamic-slice_bitcast_fusion.2), channel_id=1, source_target_pairs={{0,4},{1,5},{2,6},{3,7},{4,0},{5,1},{6,2},{7,3},{8,12},{9,13},{10,... | collective-permute-start | bytes 6291464 | tf_op jit(solution)/shard_map/ppermute | solution.py:305
  365.0 49.3 %collective-permute-start.67 = (bf16[2,2,4,32,2048]{4,3,2,1,0:T(8,128)(2,1)}, bf16[2,2,4,32,2048]{4,3,2,1,0:T(8,128)(2,1)}, u32[]{:S(2)}, u32[]{:S(2)}) collective-permute-start(bf16[2,2,4,32,2048]{4,3,2,1,0:T(8,128)(2,1)} %dynamic-slice_bitcast_fusion.1), channel_id=1, source_target_pairs={{0,4},{1,5},{2,6},{3,7},{4,0},{5,1},{6,2},{7,3},{8,12},{9,13},{10,... | collective-permute-start | bytes 6291464 | tf_op jit(solution)/shard_map/ppermute | solution.py:305
  380.9 145.4 %collective-permute-start.73 = (bf16[2,2,4,32,3072]{4,3,2,1,0:T(8,128)(2,1)}, bf16[2,2,4,32,3072]{4,3,2,1,0:T(8,128)(2,1)}, u32[]{:S(2)}, u32[]{:S(2)}) collective-permute-start(bf16[2,2,4,32,3072]{4,3,2,1,0:T(8,128)(2,1)} %dynamic-slice_bitcast_fusion), channel_id=1, source_target_pairs={{0,4},{1,5},{2,6},{3,7},{4,0},{5,1},{6,2},{7,3},{8,12},{9,13},{10,... | collective-permute-start | bytes 9437192 | tf_op jit(solution)/shard_map/ppermute | solution.py:305
  380.9 151.4 %collective-permute-start.79 = (bf16[2,2,4,32,3072]{4,3,2,0,1:T(8,128)(2,1)}, bf16[2,2,4,32,3072]{4,3,2,0,1:T(8,128)(2,1)}, u32[]{:S(2)}, u32[]{:S(2)}) collective-permute-start(bf16[2,2,4,32,3072]{4,3,2,0,1:T(8,128)(2,1)} %bitcast.291), channel_id=1, source_target_pairs={{0,4},{1,5},{2,6},{3,7},{4,0},{5,1},{6,2},{7,3},{8,12},{9,13},{10,... | collective-permute-start | bytes 9437192 | tf_op jit(solution)/shard_map/ppermute | solution.py:305
  403.3 94.5 %collective-permute-start.53 = (bf16[256,1024]{1,0:T(8,128)(2,1)}, bf16[256,1024]{1,0:T(8,128)(2,1)}, u32[]{:S(2)}, u32[]{:S(2)}) collective-permute-start(bf16[256,1024]{1,0:T(8,128)(2,1)} %get-tuple-element.75), channel_id=1, source_target_pairs={{0,0},{1,3},{2,4},{3,7},{4,1},{5,2},{6,5},{7,6},{8,8},{9,11},{10,1... | collective-permute-start | bytes 1572872 | tf_op jit(solution)/shard_map/ppermute | solution.py:305
  408.7 90.7 %collective-permute-start.54 = (bf16[256,1024]{1,0:T(8,128)(2,1)}, bf16[256,1024]{1,0:T(8,128)(2,1)}, u32[]{:S(2)}, u32[]{:S(2)}) collective-permute-start(bf16[256,1024]{1,0:T(8,128)(2,1)} %get-tuple-element.76), channel_id=1, source_target_pairs={{0,3},{1,0},{2,7},{3,4},{4,2},{5,1},{6,6},{7,5},{8,11},{9,8},{10,1... | collective-permute-start | bytes 1572872 | tf_op jit(solution)/shard_map/ppermute | solution.py:305
  414.3 88.7 %collective-permute-start.56 = (bf16[2,4,32,2048]{3,2,1,0:T(8,128)(2,1)}, bf16[2,4,32,2048]{3,2,1,0:T(8,128)(2,1)}, u32[]{:S(2)}, u32[]{:S(2)}) collective-permute-start(bf16[2,4,32,2048]{3,2,1,0:T(8,128)(2,1)} %dynamic-slice_bitcast_fusion.8), channel_id=1, source_target_pairs={{0,16},{1,17},{2,18},{3,19},{4,20},{5,21},{6,22},{7,23},{8,24},{9,... | collective-permute-start | bytes 3145736 | tf_op jit(solution)/shard_map/ppermute | solution.py:305
  499.4 36.9 %collective-permute-start.85 = (bf16[2,2,4,32,3072]{4,3,2,0,1:T(8,128)(2,1)S(1)}, bf16[2,2,4,32,3072]{4,3,2,0,1:T(8,128)(2,1)S(1)}, u32[]{:S(2)}, u32[]{:S(2)}) collective-permute-start(bf16[2,2,4,32,3072]{4,3,2,0,1:T(8,128)(2,1)S(1)} %bitcast.326), channel_id=1, source_target_pairs={{0,4},{1,5},{2,6},{3,7},{4,0},{5,1},{6,2},{7,3},{8,12},{9,13},{10,... | collective-permute-start | bytes 9437192 | tf_op jit(solution)/shard_map/ppermute | solution.py:305
  503.0 62.8 %collective-permute-start.61 = (bf16[2,2,4,32,2048]{4,3,2,0,1:T(8,128)(2,1)S(1)}, bf16[2,2,4,32,2048]{4,3,2,0,1:T(8,128)(2,1)S(1)}, u32[]{:S(2)}, u32[]{:S(2)}) collective-permute-start(bf16[2,2,4,32,2048]{4,3,2,0,1:T(8,128)(2,1)S(1)} %bitcast.329), channel_id=1, source_target_pairs={{0,4},{1,5},{2,6},{3,7},{4,0},{5,1},{6,2},{7,3},{8,12},{9,13},{10,... | collective-permute-start | bytes 6291464 | tf_op jit(solution)/shard_map/ppermute | solution.py:305
  532.3 35.4 %collective-permute-start.74 = (bf16[2,4,32,3072]{3,2,1,0:T(8,128)(2,1)}, bf16[2,4,32,3072]{3,2,1,0:T(8,128)(2,1)S(1)}, u32[]{:S(2)}, u32[]{:S(2)}) collective-permute-start(bf16[2,4,32,3072]{3,2,1,0:T(8,128)(2,1)} %dynamic-slice_bitcast_fusion.5), channel_id=1, source_target_pairs={{0,16},{1,17},{2,18},{3,19},{4,20},{5,21},{6,22},{7,23},{8,24},{9,... | collective-permute-start | bytes 4718600 | tf_op jit(solution)/shard_map/ppermute | solution.py:305
  559.1 37.3 %collective-permute-start.80 = (bf16[2,4,32,3072]{3,2,1,0:T(8,128)(2,1)S(1)}, bf16[2,4,32,3072]{3,2,1,0:T(8,128)(2,1)S(1)}, u32[]{:S(2)}, u32[]{:S(2)}) collective-permute-start(bf16[2,4,32,3072]{3,2,1,0:T(8,128)(2,1)S(1)} %dynamic-slice_bitcast_fusion.4), channel_id=1, source_target_pairs={{0,8},{1,9},{2,10},{3,11},{4,12},{5,13},{6,14},{7,15},{8,0},{9,1},... | collective-permute-start | bytes 4718600 | tf_op jit(solution)/shard_map/ppermute | solution.py:305
  563.5 66.5 %collective-permute-start.86 = (bf16[2,4,32,3072]{3,2,1,0:T(8,128)(2,1)S(1)}, bf16[2,4,32,3072]{3,2,1,0:T(8,128)(2,1)S(1)}, u32[]{:S(2)}, u32[]{:S(2)}) collective-permute-start(bf16[2,4,32,3072]{3,2,1,0:T(8,128)(2,1)S(1)} %dynamic-slice_bitcast_fusion.3), channel_id=1, source_target_pairs={{0,8},{1,9},{2,10},{3,11},{4,12},{5,13},{6,14},{7,15},{8,0},{9,1},... | collective-permute-start | bytes 4718600 | tf_op jit(solution)/shard_map/ppermute | solution.py:305
  566.7 85.9 %collective-permute-start.62 = (bf16[2,4,32,2048]{3,2,1,0:T(8,128)(2,1)S(1)}, bf16[2,4,32,2048]{3,2,1,0:T(8,128)(2,1)S(1)}, u32[]{:S(2)}, u32[]{:S(2)}) collective-permute-start(bf16[2,4,32,2048]{3,2,1,0:T(8,128)(2,1)S(1)} %dynamic-slice_bitcast_fusion.7), channel_id=1, source_target_pairs={{0,8},{1,9},{2,10},{3,11},{4,12},{5,13},{6,14},{7,15},{8,0},{9,1},... | collective-permute-start | bytes 3145736 | tf_op jit(solution)/shard_map/ppermute | solution.py:305
  568.4 96.0 %collective-permute-start.75 = (bf16[4,32,3072]{2,1,0:T(8,128)(2,1)S(1)}, bf16[4,32,3072]{2,1,0:T(8,128)(2,1)S(1)}, u32[]{:S(2)}, u32[]{:S(2)}) collective-permute-start(bf16[4,32,3072]{2,1,0:T(8,128)(2,1)S(1)} %dynamic-slice_bitcast_fusion.11), channel_id=1, source_target_pairs={{0,8},{1,9},{2,10},{3,11},{4,12},{5,13},{6,14},{7,15},{8,0},{9,1},... | collective-permute-start | bytes 2359304 | tf_op jit(solution)/shard_map/ppermute | solution.py:305
  597.0 71.1 %collective-permute-start.81 = (bf16[4,32,3072]{2,1,0:T(8,128)(2,1)S(1)}, bf16[4,32,3072]{2,1,0:T(8,128)(2,1)S(1)}, u32[]{:S(2)}, u32[]{:S(2)}) collective-permute-start(bf16[4,32,3072]{2,1,0:T(8,128)(2,1)S(1)} %dynamic-slice_bitcast_fusion.10), channel_id=1, source_target_pairs={{0,16},{1,17},{2,18},{3,19},{4,20},{5,21},{6,22},{7,23},{8,24},{9,... | collective-permute-start | bytes 2359304 | tf_op jit(solution)/shard_map/ppermute | solution.py:305
  630.8 38.3 %collective-permute-start.87 = (bf16[4,32,3072]{2,1,0:T(8,128)(2,1)S(1)}, bf16[4,32,3072]{2,1,0:T(8,128)(2,1)S(1)}, u32[]{:S(2)}, u32[]{:S(2)}) collective-permute-start(bf16[4,32,3072]{2,1,0:T(8,128)(2,1)S(1)} %dynamic-slice_bitcast_fusion.9), channel_id=1, source_target_pairs={{0,16},{1,17},{2,18},{3,19},{4,20},{5,21},{6,22},{7,23},{8,24},{9,... | collective-permute-start | bytes 2359304 | tf_op jit(solution)/shard_map/ppermute | solution.py:305
  653.0 49.8 %collective-permute-start.63 = (bf16[4,32,2048]{2,1,0:T(8,128)(2,1)S(1)}, bf16[4,32,2048]{2,1,0:T(8,128)(2,1)S(1)}, u32[]{:S(2)}, u32[]{:S(2)}) collective-permute-start(bf16[4,32,2048]{2,1,0:T(8,128)(2,1)S(1)} %dynamic-slice_bitcast_fusion.13), channel_id=1, source_target_pairs={{0,16},{1,17},{2,18},{3,19},{4,20},{5,21},{6,22},{7,23},{8,24},{9,... | collective-permute-start | bytes 1572872 | tf_op jit(solution)/shard_map/ppermute | solution.py:305
  (132 other events, 1945.6 us)
